TPU v7x, 512 devices: a whole 4x4x16 slice. The times are simulated.
512 devices in a mesh: gx: 16 (over z), gy: 8 (over y, core), gz: 4 (over x).
Axes of the slice: x: 4, y: 4, z: 16, core: 2. Of those that a mesh axis runs over, the one named last changes fastest.
Arguments:
- rhs: float32 [256, 256, 512], P('gx', 'gy', 'gz'), may hold values from -8 to 8
- kappa: float32 [256, 256, 512], P('gx', 'gy', 'gz'), may hold values from 0.1 to 10
Outputs:
- pressure: float32 [256, 256, 512], P('gx', 'gy', 'gz')
- residual: float32 [256, 256, 512], P('gx', 'gy', 'gz')
All inputs are finite; a program needn't handle non-finite values.
Results may differ from a plain program's by a relative error of at most 0.0003.
Values sent between devices are 32-bit elements; how exact they have to be, the bound alone decides.
A program may use at most 128 MiB of HBM per device.

v0:
```python
import jax
import jax.numpy as jnp
from jax import lax
from jax.sharding import PartitionSpec as P

COARSE_SWEEPS = 8


OMEGA = 0.8


def with_halo(cells, sides, width):
    for axis, dim in sides:
        count = lax.axis_size(axis)
        ends = count - 1
        head = lax.slice_in_dim(cells, 0, width, axis=dim)
        tail = lax.slice_in_dim(cells, cells.shape[dim] - width, cells.shape[dim], axis=dim)
        cells = jnp.concatenate(
            [
                lax.ppermute(tail, axis, [(i, (i + 1) % count) for i in range(ends)]),
                cells,
                lax.ppermute(head, axis, [((i + 1) % count, i) for i in range(ends)]),
            ],
            axis=dim,
        )
    return cells


def neighbours(padded):
    return [
        padded[:-2, 1:-1, 1:-1],
        padded[2:, 1:-1, 1:-1],
        padded[1:-1, :-2, 1:-1],
        padded[1:-1, 2:, 1:-1],
        padded[1:-1, 1:-1, :-2],
        padded[1:-1, 1:-1, 2:],
    ]


def face_weights(kappa_padded, scale):
    centre = kappa_padded[1:-1, 1:-1, 1:-1]
    weights = [scale * 0.5 * (centre + other) for other in neighbours(kappa_padded)]
    diag = weights[0] + weights[1] + weights[2] + weights[3] + weights[4] + weights[5]
    return (weights, diag)


def apply_padded(field, padded, weights, diag):
    others = neighbours(padded)
    total = weights[0] * others[0]
    for index in range(1, 6):
        total = total + weights[index] * others[index]
    return diag * field - total


def restrict(field):
    a, b, c = field.shape
    return field.reshape(a // 2, 2, b // 2, 2, c // 2, 2).mean(axis=(1, 3, 5))


def prolong(field):
    return jnp.repeat(jnp.repeat(jnp.repeat(field, 2, axis=0), 2, axis=1), 2, axis=2)


def level_weights(kappa_block, scale):
    padded = with_halo(kappa_block, (("gx", 0), ("gy", 1), ("gz", 2)), 1)
    return face_weights(padded, scale)


def operate(field, weights, diag):
    padded = with_halo(field, (("gx", 0), ("gy", 1), ("gz", 2)), 1)
    return apply_padded(field, padded, weights, diag)


def sweep(field, source, weights, diag):
    return field + OMEGA * (source - operate(field, weights, diag)) / diag


def body(rhs, kappa):
    kappas = [kappa]
    for level in range(3):
        kappas.append(restrict(kappas[-1]))
    levels = [level_weights(kappas[level], 0.25**level) for level in range(2)]
    sources = [rhs]
    iterates = []
    for level in range(2):
        weights, diag = levels[level]
        source = sources[level]
        field = OMEGA * source / diag
        field = sweep(field, source, weights, diag)
        iterates.append(field)
        sources.append(restrict(source - operate(field, weights, diag)))
    weights2, diag2 = level_weights(kappas[2], 0.25**2)
    field2 = OMEGA * sources[2] / diag2
    field2 = sweep(field2, sources[2], weights2, diag2)
    source3 = restrict(sources[2] - operate(field2, weights2, diag2))
    weights, diag = level_weights(kappas[3], 0.25**3)
    coarse = OMEGA * source3 / diag
    for step in range(COARSE_SWEEPS - 1):
        coarse = sweep(coarse, source3, weights, diag)
    field2 = field2 + prolong(coarse)
    field2 = sweep(field2, sources[2], weights2, diag2)
    field2 = sweep(field2, sources[2], weights2, diag2)
    coarse = field2
    for level in (1, 0):
        weights, diag = levels[level]
        field = iterates[level] + prolong(coarse)
        field = sweep(field, sources[level], weights, diag)
        field = sweep(field, sources[level], weights, diag)
        coarse = field
    weights, diag = levels[0]
    return (coarse, rhs - operate(coarse, weights, diag))


def solution(mesh):
    placed = (P("gx", "gy", "gz"), P("gx", "gy", "gz"))
    return jax.shard_map(
        body,
        mesh=mesh,
        in_specs=placed,
        out_specs=(P("gx", "gy", "gz"), P("gx", "gy", "gz")),
        check_vma=False,
    )
```

profile of v0, /device:TPU:1, one launch (start us, length us, event | category | flops | bytes accessed | tf_op | source)
XLA Modules:
  0.0 656.7 jit_solution(1340945841622318917)
XLA Ops:
  2.7 5.1 collective-permute-start
  7.8 18.8 %reshape.52 = f32[8,2,16,2,64,2]{5,4,3,2,1,0:T(8,128)} reshape(f32[16,32,128]{2,1,0:T(8,128)} %param.3) | data formatting | bytes 524288 | tf_op jit(solution)/shard_map/reshape | solution.py:57
  26.7 7.0 %reduce_sum.55 = f32[8,16,64]{2,1,0:T(8,128)S(1)} reduce(f32[8,2,16,2,64,2]{5,4,3,2,1,0:T(8,128)} %reshape.52, f32[]{:T(128)} %constant.11.clone.1), dimensions={1,3,5}, to_apply=%region_1.0 | reduce | flops 57344 | bytes 294916 | tf_op jit(solution)/shard_map/reduce_sum | solution.py:57
  33.8 8.3 %collective-permute-start.3 = (f32[18,1,128]{2,1,0:T(1,128)S(1)}, f32[18,1,128]{2,1,0:T(1,128)S(1)}, u32[]{:S(2)}, u32[]{:S(2)}) collective-permute-start(f32[18,1,128]{2,1,0:T(1,128)S(1)} %get-tuple-element.52), channel_id=1, source_target_pairs={{4,0},{8,4},{12,8},{16,12},{20,16},{24,20},{28,24},{5,1},{9,5},{13... | collective-permute-start | bytes 27656 | tf_op jit(solution)/shard_map/ppermute | solution.py:22
  56.2 4.0 collective-permute-start.4
  60.3 5.6 collective-permute-done.5
  73.9 5.2 collective-permute-start.8
  81.1 4.6 collective-permute-start.36
  85.9 4.1 collective-permute-start.10
  91.3 5.3 collective-permute-done.10
  96.7 4.1 collective-permute-done.11
  108.2 5.2 collective-permute-start.20
  127.5 5.3 collective-permute-start.22
  132.8 4.0 collective-permute-done.17
  137.2 18.1 %reshape.51 = f32[8,2,16,2,64,2]{5,4,3,2,1,0:T(8,128)} reshape(f32[16,32,128]{2,1,0:T(8,128)S(1)} %fusion.48) | data formatting | bytes 524288 | tf_op jit(solution)/shard_map/reshape | solution.py:57
  155.3 7.0 %reduce_sum.54 = f32[8,16,64]{2,1,0:T(8,128)S(1)} reduce(f32[8,2,16,2,64,2]{5,4,3,2,1,0:T(8,128)} %reshape.51, f32[]{:T(128)} %constant.11.clone.1), dimensions={1,3,5}, to_apply=%region_0.0 | reduce | flops 57344 | bytes 294916 | tf_op jit(solution)/shard_map/reduce_sum | solution.py:57
  163.4 4.3 collective-permute-start.24
  187.0 4.1 collective-permute-done.29
  191.3 4.3 collective-permute-start.30
  197.0 4.6 collective-permute-done.31
  201.5 4.4 collective-permute-start.32
  226.7 4.8 collective-permute-start.42
  232.9 5.0 collective-permute-start.54
  239.3 6.2 collective-permute-start.44
  247.5 4.6 collective-permute-done.45
  284.1 4.6 collective-permute-start.58
  298.3 4.5 collective-permute-start.62
  316.7 4.8 collective-permute-start.66
  326.2 4.2 collective-permute-start.68
  351.6 4.8 collective-permute-start.74
  375.1 4.8 collective-permute-start.80
  391.2 4.3 collective-permute-start.84
  400.1 4.5 collective-permute-start.86
  424.1 4.5 collective-permute-start.92
  447.9 4.8 collective-permute-start.98
  471.8 4.5 collective-permute-start.104
  496.1 4.5 collective-permute-start.110
  521.3 4.2 collective-permute-start.116
  546.2 4.7 collective-permute-start.122
  572.2 4.6 collective-permute-start.128
  585.0 5.6 collective-permute-done.130
  590.7 4.1 collective-permute-done.131
  602.6 4.4 collective-permute-start.134
  615.4 5.6 collective-permute-done.136
  621.0 4.1 collective-permute-done.137
  633.0 4.4 collective-permute-start.140
  645.8 5.6 collective-permute-done.142
  651.4 4.1 collective-permute-done.143
  (424 shorter events, 392.7 us)
Async XLA Ops:
  1.4 32.4 %collective-permute-start.1 = (f32[1,32,128]{2,1,0:T(8,128)S(1)}, f32[1,32,128]{2,1,0:T(8,128)S(1)}, u32[]{:S(2)}, u32[]{:S(2)}) collective-permute-start(f32[1,32,128]{2,1,0:T(8,128)S(1)} %get-tuple-element.64), channel_id=1, source_target_pairs={{32,0},{64,32},{96,64},{128,96},{160,128},{192,160},{224,192},{256... | collective-permute-start | bytes 49160 | tf_op jit(solution)/shard_map/ppermute | solution.py:22
  2.7 31.0 %collective-permute-start = (f32[1,32,128]{2,1,0:T(8,128)S(1)}, f32[1,32,128]{2,1,0:T(8,128)S(1)}, u32[]{:S(2)}, u32[]{:S(2)}) collective-permute-start(f32[1,32,128]{2,1,0:T(8,128)S(1)} %get-tuple-element.65), channel_id=1, source_target_pairs={{0,32},{32,64},{64,96},{96,128},{128,160},{160,192},{192,224},{224... | collective-permute-start | bytes 49160 | tf_op jit(solution)/shard_map/ppermute | solution.py:20
  33.8 20.9 %collective-permute-start.3 = (f32[18,1,128]{2,1,0:T(1,128)S(1)}, f32[18,1,128]{2,1,0:T(1,128)S(1)}, u32[]{:S(2)}, u32[]{:S(2)}) collective-permute-start(f32[18,1,128]{2,1,0:T(1,128)S(1)} %get-tuple-element.52), channel_id=1, source_target_pairs={{4,0},{8,4},{12,8},{16,12},{20,16},{24,20},{28,24},{5,1},{9,5},{13... | collective-permute-start | bytes 27656 | tf_op jit(solution)/shard_map/ppermute | solution.py:22
  42.1 12.6 %collective-permute-start.2 = (f32[18,1,128]{2,1,0:T(1,128)S(1)}, f32[18,1,128]{2,1,0:T(1,128)S(1)}, u32[]{:S(2)}, u32[]{:S(2)}) collective-permute-start(f32[18,1,128]{2,1,0:T(1,128)S(1)} %get-tuple-element.53), channel_id=1, source_target_pairs={{0,4},{4,8},{8,12},{12,16},{16,20},{20,24},{24,28},{1,5},{5,9},{9,... | collective-permute-start | bytes 27656 | tf_op jit(solution)/shard_map/ppermute | solution.py:20
  44.1 62.2 %collective-permute-start.19 = (f32[1,16,64]{2,1,0:T(8,128)S(1)}, f32[1,16,64]{2,1,0:T(8,128)S(1)}, u32[]{:S(2)}, u32[]{:S(2)}) collective-permute-start(f32[1,16,64]{2,1,0:T(8,128)S(1)} %get-tuple-element.94), channel_id=1, source_target_pairs={{32,0},{64,32},{96,64},{128,96},{160,128},{192,160},{224,192},{256... | collective-permute-start | bytes 12296 | tf_op jit(solution)/shard_map/ppermute | solution.py:22
  45.4 60.9 %collective-permute-start.18 = (f32[1,16,64]{2,1,0:T(8,128)S(1)}, f32[1,16,64]{2,1,0:T(8,128)S(1)}, u32[]{:S(2)}, u32[]{:S(2)}) collective-permute-start(f32[1,16,64]{2,1,0:T(8,128)S(1)} %get-tuple-element.95), channel_id=1, source_target_pairs={{0,32},{32,64},{64,96},{96,128},{128,160},{160,192},{192,224},{224... | collective-permute-start | bytes 12296 | tf_op jit(solution)/shard_map/ppermute | solution.py:20
  54.9 10.9 %collective-permute-start.5 = (f32[18,34,1]{2,1,0:T(8,128)S(1)}, f32[18,34,1]{2,1,0:T(8,128)S(1)}, u32[]{:S(2)}, u32[]{:S(2)}) collective-permute-start(f32[18,34,1]{2,1,0:T(8,128)S(1)} %get-tuple-element.40), channel_id=1, source_target_pairs={{1,0},{2,1},{3,2},{5,4},{6,5},{7,6},{9,8},{10,9},{11,10},{13,12},{... | collective-permute-start | bytes 7352 | tf_op jit(solution)/shard_map/ppermute | solution.py:22
  56.2 10.5 %collective-permute-start.4 = (f32[18,34,1]{2,1,0:T(8,128)S(1)}, f32[18,34,1]{2,1,0:T(8,128)S(1)}, u32[]{:S(2)}, u32[]{:S(2)}) collective-permute-start(f32[18,34,1]{2,1,0:T(8,128)S(1)} %get-tuple-element.41), channel_id=1, source_target_pairs={{0,1},{1,2},{2,3},{4,5},{5,6},{6,7},{8,9},{9,10},{10,11},{12,13},{... | collective-permute-start | bytes 7352 | tf_op jit(solution)/shard_map/ppermute | solution.py:20
  70.7 19.3 %collective-permute-start.37 = (f32[1,8,32]{2,1,0:T(8,128)S(1)}, f32[1,8,32]{2,1,0:T(8,128)S(1)}, u32[]{:S(2)}, u32[]{:S(2)}) collective-permute-start(f32[1,8,32]{2,1,0:T(8,128)S(1)} %get-tuple-element.150), channel_id=1, source_target_pairs={{32,0},{64,32},{96,64},{128,96},{160,128},{192,160},{224,192},{256... | collective-permute-start | bytes 3080 | tf_op jit(solution)/shard_map/ppermute | solution.py:22
  73.9 7.2 %collective-permute-start.8 = (f32[18,1,128]{2,1,0:T(1,128)S(1)}, f32[18,1,128]{2,1,0:T(1,128)S(1)}, u32[]{:S(2)}, u32[]{:S(2)}) collective-permute-start(f32[18,1,128]{2,1,0:T(1,128)S(1)} %get-tuple-element.50), channel_id=1, source_target_pairs={{0,4},{4,8},{8,12},{12,16},{16,20},{20,24},{24,28},{1,5},{5,9},{9,... | collective-permute-start | bytes 27656 | tf_op jit(solution)/shard_map/ppermute | solution.py:20
  81.1 10.3 %collective-permute-start.36 = (f32[1,8,32]{2,1,0:T(8,128)S(1)}, f32[1,8,32]{2,1,0:T(8,128)S(1)}, u32[]{:S(2)}, u32[]{:S(2)}) collective-permute-start(f32[1,8,32]{2,1,0:T(8,128)S(1)} %get-tuple-element.151), channel_id=1, source_target_pairs={{0,32},{32,64},{64,96},{96,128},{128,160},{160,192},{192,224},{224... | collective-permute-start | bytes 3080 | tf_op jit(solution)/shard_map/ppermute | solution.py:20
  85.9 10.8 %collective-permute-start.10 = (f32[18,34,1]{2,1,0:T(8,128)S(1)}, f32[18,34,1]{2,1,0:T(8,128)S(1)}, u32[]{:S(2)}, u32[]{:S(2)}) collective-permute-start(f32[18,34,1]{2,1,0:T(8,128)S(1)} %get-tuple-element.38), channel_id=1, source_target_pairs={{0,1},{1,2},{2,3},{4,5},{5,6},{6,7},{8,9},{9,10},{10,11},{12,13},{... | collective-permute-start | bytes 7352 | tf_op jit(solution)/shard_map/ppermute | solution.py:20
  90.0 10.8 %collective-permute-start.11 = (f32[18,34,1]{2,1,0:T(8,128)S(1)}, f32[18,34,1]{2,1,0:T(8,128)S(1)}, u32[]{:S(2)}, u32[]{:S(2)}) collective-permute-start(f32[18,34,1]{2,1,0:T(8,128)S(1)} %get-tuple-element.39), channel_id=1, source_target_pairs={{1,0},{2,1},{3,2},{5,4},{6,5},{7,6},{9,8},{10,9},{11,10},{13,12},{... | collective-permute-start | bytes 7352 | tf_op jit(solution)/shard_map/ppermute | solution.py:22
  101.3 12.1 %collective-permute-start.12 = (f32[1,32,128]{2,1,0:T(8,128)S(1)}, f32[1,32,128]{2,1,0:T(8,128)S(1)}, u32[]{:S(2)}, u32[]{:S(2)}) collective-permute-start(f32[1,32,128]{2,1,0:T(8,128)S(1)} %get-tuple-element.60), channel_id=1, source_target_pairs={{0,32},{32,64},{64,96},{96,128},{128,160},{160,192},{192,224},{224... | collective-permute-start | bytes 49160 | tf_op jit(solution)/shard_map/ppermute | solution.py:20
  104.9 8.5 %collective-permute-start.13 = (f32[1,32,128]{2,1,0:T(8,128)S(1)}, f32[1,32,128]{2,1,0:T(8,128)S(1)}, u32[]{:S(2)}, u32[]{:S(2)}) collective-permute-start(f32[1,32,128]{2,1,0:T(8,128)S(1)} %get-tuple-element.61), channel_id=1, source_target_pairs={{32,0},{64,32},{96,64},{128,96},{160,128},{192,160},{224,192},{256... | collective-permute-start | bytes 49160 | tf_op jit(solution)/shard_map/ppermute | solution.py:22
  106.3 11.5 %collective-permute-start.21 = (f32[10,1,64]{2,1,0:T(1,128)S(1)}, f32[10,1,64]{2,1,0:T(1,128)S(1)}, u32[]{:S(2)}, u32[]{:S(2)}) collective-permute-start(f32[10,1,64]{2,1,0:T(1,128)S(1)} %get-tuple-element.84), channel_id=1, source_target_pairs={{4,0},{8,4},{12,8},{16,12},{20,16},{24,20},{28,24},{5,1},{9,5},{13... | collective-permute-start | bytes 7688 | tf_op jit(solution)/shard_map/ppermute | solution.py:22
  108.2 9.6 %collective-permute-start.20 = (f32[10,1,64]{2,1,0:T(1,128)S(1)}, f32[10,1,64]{2,1,0:T(1,128)S(1)}, u32[]{:S(2)}, u32[]{:S(2)}) collective-permute-start(f32[10,1,64]{2,1,0:T(1,128)S(1)} %get-tuple-element.85), channel_id=1, source_target_pairs={{0,4},{4,8},{8,12},{12,16},{16,20},{20,24},{24,28},{1,5},{5,9},{9,... | collective-permute-start | bytes 7688 | tf_op jit(solution)/shard_map/ppermute | solution.py:20
  121.1 11.7 %collective-permute-start.16 = (f32[18,34,1]{2,1,0:T(8,128)S(1)}, f32[18,34,1]{2,1,0:T(8,128)S(1)}, u32[]{:S(2)}, u32[]{:S(2)}) collective-permute-start(f32[18,34,1]{2,1,0:T(8,128)S(1)} %get-tuple-element.36), channel_id=1, source_target_pairs={{0,1},{1,2},{2,3},{4,5},{5,6},{6,7},{8,9},{9,10},{10,11},{12,13},{... | collective-permute-start | bytes 7352 | tf_op jit(solution)/shard_map/ppermute | solution.py:20
  124.2 12.6 %collective-permute-start.17 = (f32[18,34,1]{2,1,0:T(8,128)S(1)}, f32[18,34,1]{2,1,0:T(8,128)S(1)}, u32[]{:S(2)}, u32[]{:S(2)}) collective-permute-start(f32[18,34,1]{2,1,0:T(8,128)S(1)} %get-tuple-element.37), channel_id=1, source_target_pairs={{1,0},{2,1},{3,2},{5,4},{6,5},{7,6},{9,8},{10,9},{11,10},{13,12},{... | collective-permute-start | bytes 7352 | tf_op jit(solution)/shard_map/ppermute | solution.py:22
  126.2 36.1 %collective-permute-start.23 = (f32[10,18,1]{2,1,0:T(8,128)}, f32[10,18,1]{2,1,0:T(8,128)}, u32[]{:S(2)}, u32[]{:S(2)}) collective-permute-start(f32[10,18,1]{2,1,0:T(8,128)} %get-tuple-element.74), channel_id=1, source_target_pairs={{1,0},{2,1},{3,2},{5,4},{6,5},{7,6},{9,8},{10,9},{11,10},{13,12},{... | collective-permute-start | bytes 2168 | tf_op jit(solution)/shard_map/ppermute | solution.py:22
  127.5 34.8 %collective-permute-start.22 = (f32[10,18,1]{2,1,0:T(8,128)}, f32[10,18,1]{2,1,0:T(8,128)}, u32[]{:S(2)}, u32[]{:S(2)}) collective-permute-start(f32[10,18,1]{2,1,0:T(8,128)} %get-tuple-element.75), channel_id=1, source_target_pairs={{0,1},{1,2},{2,3},{4,5},{5,6},{6,7},{8,9},{9,10},{10,11},{12,13},{... | collective-permute-start | bytes 2168 | tf_op jit(solution)/shard_map/ppermute | solution.py:20
  163.4 11.2 %collective-permute-start.24 = (f32[1,16,64]{2,1,0:T(8,128)S(1)}, f32[1,16,64]{2,1,0:T(8,128)S(1)}, u32[]{:S(2)}, u32[]{:S(2)}) collective-permute-start(f32[1,16,64]{2,1,0:T(8,128)S(1)} %get-tuple-element.92), channel_id=1, source_target_pairs={{0,32},{32,64},{64,96},{96,128},{128,160},{160,192},{192,224},{224... | collective-permute-start | bytes 12296 | tf_op jit(solution)/shard_map/ppermute | solution.py:20
  167.8 6.9 %collective-permute-start.25 = (f32[1,16,64]{2,1,0:T(8,128)S(1)}, f32[1,16,64]{2,1,0:T(8,128)S(1)}, u32[]{:S(2)}, u32[]{:S(2)}) collective-permute-start(f32[1,16,64]{2,1,0:T(8,128)S(1)} %get-tuple-element.93), channel_id=1, source_target_pairs={{32,0},{64,32},{96,64},{128,96},{160,128},{192,160},{224,192},{256... | collective-permute-start | bytes 12296 | tf_op jit(solution)/shard_map/ppermute | solution.py:22
  169.1 27.8 %collective-permute-start.39 = (f32[6,1,32]{2,1,0:T(1,128)S(1)}, f32[6,1,32]{2,1,0:T(1,128)S(1)}, u32[]{:S(2)}, u32[]{:S(2)}) collective-permute-start(f32[6,1,32]{2,1,0:T(1,128)S(1)} %get-tuple-element.124), channel_id=1, source_target_pairs={{4,0},{8,4},{12,8},{16,12},{20,16},{24,20},{28,24},{5,1},{9,5},{13... | collective-permute-start | bytes 2312 | tf_op jit(solution)/shard_map/ppermute | solution.py:22
  171.0 8.0 %collective-permute-start.38 = (f32[6,1,32]{2,1,0:T(1,128)S(1)}, f32[6,1,32]{2,1,0:T(1,128)S(1)}, u32[]{:S(2)}, u32[]{:S(2)}) collective-permute-start(f32[6,1,32]{2,1,0:T(1,128)S(1)} %get-tuple-element.125), channel_id=1, source_target_pairs={{0,4},{4,8},{8,12},{12,16},{16,20},{20,24},{24,28},{1,5},{5,9},{9,... | collective-permute-start | bytes 2312 | tf_op jit(solution)/shard_map/ppermute | solution.py:20
  201.5 11.9 %collective-permute-start.32 = (f32[10,1,64]{2,1,0:T(1,128)S(1)}, f32[10,1,64]{2,1,0:T(1,128)S(1)}, u32[]{:S(2)}, u32[]{:S(2)}) collective-permute-start(f32[10,1,64]{2,1,0:T(1,128)S(1)} %get-tuple-element.80), channel_id=1, source_target_pairs={{0,4},{4,8},{8,12},{12,16},{16,20},{20,24},{24,28},{1,5},{5,9},{9,... | collective-permute-start | bytes 7688 | tf_op jit(solution)/shard_map/ppermute | solution.py:20
  206.0 7.5 %collective-permute-start.33 = (f32[10,1,64]{2,1,0:T(1,128)S(1)}, f32[10,1,64]{2,1,0:T(1,128)S(1)}, u32[]{:S(2)}, u32[]{:S(2)}) collective-permute-start(f32[10,1,64]{2,1,0:T(1,128)S(1)} %get-tuple-element.81), channel_id=1, source_target_pairs={{4,0},{8,4},{12,8},{16,12},{20,16},{24,20},{28,24},{5,1},{9,5},{13... | collective-permute-start | bytes 7688 | tf_op jit(solution)/shard_map/ppermute | solution.py:22
  208.0 8.9 %collective-permute-start.41 = (f32[6,10,1]{2,0,1:T(8,128)S(1)}, f32[6,10,1]{2,0,1:T(8,128)S(1)}, u32[]{:S(2)}, u32[]{:S(2)}) collective-permute-start(f32[6,10,1]{2,0,1:T(8,128)S(1)} %get-tuple-element.114), channel_id=1, source_target_pairs={{1,0},{2,1},{3,2},{5,4},{6,5},{7,6},{9,8},{10,9},{11,10},{13,12},{... | collective-permute-start | bytes 728 | tf_op jit(solution)/shard_map/ppermute | solution.py:22
  209.5 7.4 %collective-permute-start.40 = (f32[6,10,1]{2,0,1:T(8,128)S(1)}, f32[6,10,1]{2,0,1:T(8,128)S(1)}, u32[]{:S(2)}, u32[]{:S(2)}) collective-permute-start(f32[6,10,1]{2,0,1:T(8,128)S(1)} %get-tuple-element.115), channel_id=1, source_target_pairs={{0,1},{1,2},{2,3},{4,5},{5,6},{6,7},{8,9},{9,10},{10,11},{12,13},{... | collective-permute-start | bytes 728 | tf_op jit(solution)/shard_map/ppermute | solution.py:20
  226.7 12.5 %collective-permute-start.42 = (f32[1,8,32]{2,1,0:T(8,128)S(1)}, f32[1,8,32]{2,1,0:T(8,128)S(1)}, u32[]{:S(2)}, u32[]{:S(2)}) collective-permute-start(f32[1,8,32]{2,1,0:T(8,128)S(1)} %get-tuple-element.148), channel_id=1, source_target_pairs={{0,32},{32,64},{64,96},{96,128},{128,160},{160,192},{192,224},{224... | collective-permute-start | bytes 3080 | tf_op jit(solution)/shard_map/ppermute | solution.py:20
  231.6 7.7 %collective-permute-start.43 = (f32[1,8,32]{2,1,0:T(8,128)S(1)}, f32[1,8,32]{2,1,0:T(8,128)S(1)}, u32[]{:S(2)}, u32[]{:S(2)}) collective-permute-start(f32[1,8,32]{2,1,0:T(8,128)S(1)} %get-tuple-element.149), channel_id=1, source_target_pairs={{32,0},{64,32},{96,64},{128,96},{160,128},{192,160},{224,192},{256... | collective-permute-start | bytes 3080 | tf_op jit(solution)/shard_map/ppermute | solution.py:22
  232.9 12.6 %collective-permute-start.54 = (f32[1,4,16]{2,1,0:T(4,128)S(1)}, f32[1,4,16]{2,1,0:T(4,128)S(1)}, u32[]{:S(2)}, u32[]{:S(2)}) collective-permute-start(f32[1,4,16]{2,1,0:T(4,128)S(1)} %get-tuple-element.182), channel_id=1, source_target_pairs={{0,32},{32,64},{64,96},{96,128},{128,160},{160,192},{192,224},{224... | collective-permute-start | bytes 776 | tf_op jit(solution)/shard_map/ppermute | solution.py:20
  237.9 7.6 %collective-permute-start.55 = (f32[1,4,16]{2,1,0:T(4,128)S(1)}, f32[1,4,16]{2,1,0:T(4,128)S(1)}, u32[]{:S(2)}, u32[]{:S(2)}) collective-permute-start(f32[1,4,16]{2,1,0:T(4,128)S(1)} %get-tuple-element.183), channel_id=1, source_target_pairs={{32,0},{64,32},{96,64},{128,96},{160,128},{192,160},{224,192},{256... | collective-permute-start | bytes 776 | tf_op jit(solution)/shard_map/ppermute | solution.py:22
  239.3 8.2 %collective-permute-start.44 = (f32[6,1,32]{2,1,0:T(1,128)S(1)}, f32[6,1,32]{2,1,0:T(1,128)S(1)}, u32[]{:S(2)}, u32[]{:S(2)}) collective-permute-start(f32[6,1,32]{2,1,0:T(1,128)S(1)} %get-tuple-element.122), channel_id=1, source_target_pairs={{0,4},{4,8},{8,12},{12,16},{16,20},{20,24},{24,28},{1,5},{5,9},{9,... | collective-permute-start | bytes 2312 | tf_op jit(solution)/shard_map/ppermute | solution.py:20
  252.2 8.5 %collective-permute-start.46 = (f32[6,10,1]{2,0,1:T(8,128)S(1)}, f32[6,10,1]{2,0,1:T(8,128)S(1)}, u32[]{:S(2)}, u32[]{:S(2)}) collective-permute-start(f32[6,10,1]{2,0,1:T(8,128)S(1)} %get-tuple-element.110), channel_id=1, source_target_pairs={{0,1},{1,2},{2,3},{4,5},{5,6},{6,7},{8,9},{9,10},{10,11},{12,13},{... | collective-permute-start | bytes 728 | tf_op jit(solution)/shard_map/ppermute | solution.py:20
  253.8 6.9 %collective-permute-start.47 = (f32[6,10,1]{2,0,1:T(8,128)S(1)}, f32[6,10,1]{2,0,1:T(8,128)S(1)}, u32[]{:S(2)}, u32[]{:S(2)}) collective-permute-start(f32[6,10,1]{2,0,1:T(8,128)S(1)} %get-tuple-element.111), channel_id=1, source_target_pairs={{1,0},{2,1},{3,2},{5,4},{6,5},{7,6},{9,8},{10,9},{11,10},{13,12},{... | collective-permute-start | bytes 728 | tf_op jit(solution)/shard_map/ppermute | solution.py:22
  255.1 10.9 %collective-permute-start.57 = (f32[4,1,16]{2,1,0:T(1,128)S(1)}, f32[4,1,16]{2,1,0:T(1,128)S(1)}, u32[]{:S(2)}, u32[]{:S(2)}) collective-permute-start(f32[4,1,16]{2,1,0:T(1,128)S(1)} %get-tuple-element.166), channel_id=1, source_target_pairs={{4,0},{8,4},{12,8},{16,12},{20,16},{24,20},{28,24},{5,1},{9,5},{13... | collective-permute-start | bytes 776 | tf_op jit(solution)/shard_map/ppermute | solution.py:22
  257.0 9.0 %collective-permute-start.56 = (f32[4,1,16]{2,1,0:T(1,128)S(1)}, f32[4,1,16]{2,1,0:T(1,128)S(1)}, u32[]{:S(2)}, u32[]{:S(2)}) collective-permute-start(f32[4,1,16]{2,1,0:T(1,128)S(1)} %get-tuple-element.167), channel_id=1, source_target_pairs={{0,4},{4,8},{8,12},{12,16},{16,20},{20,24},{24,28},{1,5},{5,9},{9,... | collective-permute-start | bytes 776 | tf_op jit(solution)/shard_map/ppermute | solution.py:20
  277.5 11.2 %collective-permute-start.52 = (f32[6,10,1]{2,0,1:T(8,128)S(1)}, f32[6,10,1]{2,0,1:T(8,128)S(1)}, u32[]{:S(2)}, u32[]{:S(2)}) collective-permute-start(f32[6,10,1]{2,0,1:T(8,128)S(1)} %get-tuple-element.106), channel_id=1, source_target_pairs={{0,1},{1,2},{2,3},{4,5},{5,6},{6,7},{8,9},{9,10},{10,11},{12,13},{... | collective-permute-start | bytes 728 | tf_op jit(solution)/shard_map/ppermute | solution.py:20
  281.5 7.2 %collective-permute-start.53 = (f32[6,10,1]{2,0,1:T(8,128)S(1)}, f32[6,10,1]{2,0,1:T(8,128)S(1)}, u32[]{:S(2)}, u32[]{:S(2)}) collective-permute-start(f32[6,10,1]{2,0,1:T(8,128)S(1)} %get-tuple-element.107), channel_id=1, source_target_pairs={{1,0},{2,1},{3,2},{5,4},{6,5},{7,6},{9,8},{10,9},{11,10},{13,12},{... | collective-permute-start | bytes 728 | tf_op jit(solution)/shard_map/ppermute | solution.py:22
  351.6 6.8 %collective-permute-start.74 = (f32[4,1,16]{2,1,0:T(1,128)S(1)}, f32[4,1,16]{2,1,0:T(1,128)S(1)}, u32[]{:S(2)}, u32[]{:S(2)}) collective-permute-start(f32[4,1,16]{2,1,0:T(1,128)S(1)} %get-tuple-element.160), channel_id=1, source_target_pairs={{0,4},{4,8},{8,12},{12,16},{16,20},{20,24},{24,28},{1,5},{5,9},{9,... | collective-permute-start | bytes 776 | tf_op jit(solution)/shard_map/ppermute | solution.py:20
  375.1 6.8 %collective-permute-start.80 = (f32[4,1,16]{2,1,0:T(1,128)S(1)}, f32[4,1,16]{2,1,0:T(1,128)S(1)}, u32[]{:S(2)}, u32[]{:S(2)}) collective-permute-start(f32[4,1,16]{2,1,0:T(1,128)S(1)} %get-tuple-element.158), channel_id=1, source_target_pairs={{0,4},{4,8},{8,12},{12,16},{16,20},{20,24},{24,28},{1,5},{5,9},{9,... | collective-permute-start | bytes 776 | tf_op jit(solution)/shard_map/ppermute | solution.py:20
  582.1 8.6 %collective-permute-start.130 = (f32[18,34,1]{2,1,0:T(8,128)S(1)}, f32[18,34,1]{2,1,0:T(8,128)S(1)}, u32[]{:S(2)}, u32[]{:S(2)}) collective-permute-start(f32[18,34,1]{2,1,0:T(8,128)S(1)} %get-tuple-element.34), channel_id=1, source_target_pairs={{0,1},{1,2},{2,3},{4,5},{5,6},{6,7},{8,9},{9,10},{10,11},{12,13},{... | collective-permute-start | bytes 7352 | tf_op jit(solution)/shard_map/ppermute | solution.py:20
  583.7 11.0 %collective-permute-start.131 = (f32[18,34,1]{2,1,0:T(8,128)S(1)}, f32[18,34,1]{2,1,0:T(8,128)S(1)}, u32[]{:S(2)}, u32[]{:S(2)}) collective-permute-start(f32[18,34,1]{2,1,0:T(8,128)S(1)} %get-tuple-element.35), channel_id=1, source_target_pairs={{1,0},{2,1},{3,2},{5,4},{6,5},{7,6},{9,8},{10,9},{11,10},{13,12},{... | collective-permute-start | bytes 7352 | tf_op jit(solution)/shard_map/ppermute | solution.py:22
  612.2 8.9 %collective-permute-start.136 = (f32[18,34,1]{2,1,0:T(8,128)S(1)}, f32[18,34,1]{2,1,0:T(8,128)S(1)}, u32[]{:S(2)}, u32[]{:S(2)}) collective-permute-start(f32[18,34,1]{2,1,0:T(8,128)S(1)} %get-tuple-element.32), channel_id=1, source_target_pairs={{0,1},{1,2},{2,3},{4,5},{5,6},{6,7},{8,9},{9,10},{10,11},{12,13},{... | collective-permute-start | bytes 7352 | tf_op jit(solution)/shard_map/ppermute | solution.py:20
  614.1 11.0 %collective-permute-start.137 = (f32[18,34,1]{2,1,0:T(8,128)S(1)}, f32[18,34,1]{2,1,0:T(8,128)S(1)}, u32[]{:S(2)}, u32[]{:S(2)}) collective-permute-start(f32[18,34,1]{2,1,0:T(8,128)S(1)} %get-tuple-element.33), channel_id=1, source_target_pairs={{1,0},{2,1},{3,2},{5,4},{6,5},{7,6},{9,8},{10,9},{11,10},{13,12},{... | collective-permute-start | bytes 7352 | tf_op jit(solution)/shard_map/ppermute | solution.py:22
  642.6 8.9 %collective-permute-start.142 = (f32[18,34,1]{2,1,0:T(8,128)S(1)}, f32[18,34,1]{2,1,0:T(8,128)S(1)}, u32[]{:S(2)}, u32[]{:S(2)}) collective-permute-start(f32[18,34,1]{2,1,0:T(8,128)S(1)} %get-tuple-element.30), channel_id=1, source_target_pairs={{0,1},{1,2},{2,3},{4,5},{5,6},{6,7},{8,9},{9,10},{10,11},{12,13},{... | collective-permute-start | bytes 7352 | tf_op jit(solution)/shard_map/ppermute | solution.py:20
  644.5 11.0 %collective-permute-start.143 = (f32[18,34,1]{2,1,0:T(8,128)S(1)}, f32[18,34,1]{2,1,0:T(8,128)S(1)}, u32[]{:S(2)}, u32[]{:S(2)}) collective-permute-start(f32[18,34,1]{2,1,0:T(8,128)S(1)} %get-tuple-element.31), channel_id=1, source_target_pairs={{1,0},{2,1},{3,2},{5,4},{6,5},{7,6},{9,8},{10,9},{11,10},{13,12},{... | collective-permute-start | bytes 7352 | tf_op jit(solution)/shard_map/ppermute | solution.py:22
  (99 other events, 600.2 us)
where the time goes:
time: 661 us; the launch traced here: 657 us
  starting transfers between devices  371 us (56%)
  waiting for transfers between devices  207 us (31%)
  local copies, waits for them, and re-layouts  49.7 us (8%)
  other arithmetic  25 us (4%)
    ppermute x72, starting transfers between devices, with_halo(): lax.ppermute(tail, axis, [(i, (i + 1) % count) for i in range(ends)])  256 us
    ppermute x72, waiting for transfers between devices, with_halo(): lax.ppermute(head, axis, [((i + 1) % count, i) for i in range(ends)])  181 us
    ppermute x72, starting transfers between devices, with_halo(): lax.ppermute(head, axis, [((i + 1) % count, i) for i in range(ends)])  115 us
    reshape x4, local copies, waits for them, and re-layouts, restrict(): return field.reshape(a // 2, 2, b // 2, 2, c // 2, 2).mean(axis=(1, 3, 5))  40.6 us
    ppermute x72, waiting for transfers between devices, with_halo(): lax.ppermute(tail, axis, [(i, (i + 1) % count) for i in range(ends)])  26 us
    reduce_sum x6, other arithmetic, restrict(): return field.reshape(a // 2, 2, b // 2, 2, c // 2, 2).mean(axis=(1, 3, 5))  17.8 us
  transfers between devices with their start and end apart: 144, of which 64 were waited for; matrix products, arithmetic and copies ran while one was open for 9% of the time, Pallas kernels for 0%

commit v1 on v0

v1 whole, which is shorter than its diff:
```python
import functools
import itertools

import jax
import jax.numpy as jnp
from jax import lax
from jax.experimental import pallas as pl
from jax.experimental.pallas import tpu as pltpu
from jax.sharding import PartitionSpec as P

MESH = pl.DeviceIdType.MESH
F32 = jnp.float32
OMEGA = 0.8
COARSE_SWEEPS = 8
GX, GY, GZ = 16, 8, 4
FACES = [(-1, 0, 0), (1, 0, 0), (0, -1, 0), (0, 1, 0), (0, 0, -1), (0, 0, 1)]
NEAR = [o for o in itertools.product((-1, 0, 1), repeat=3) if o != (0, 0, 0)]
FAR = [(a, b, 0) for a in (-4, -2, 0, 2, 4) for b in (-2, 0, 2) if (a, b) != (0, 0)]
PARTNERS = NEAR + FAR
ROUNDS = 5

L1 = dict(planes=18, rows=32, px=5, py=8, n=(8, 16, 64), right=72, left=120, level=1)
L2 = dict(planes=16, rows=24, px=6, py=8, n=(4, 8, 32), right=64, left=96, level=2)
L3 = dict(planes=22, rows=24, px=10, py=10, n=(2, 4, 16), right=32, left=112, level=3)

SCRATCH = {
    "ua": (18, 48, 128), "ub": (18, 48, 128), "k0": (18, 48, 128),
    "w0": (6, 16, 32, 128), "d0": (16, 32, 128), "i0": (16, 32, 128), "h0": (16, 32, 128),
    "ys": (ROUNDS, 2, 16, 128), "zs": (ROUNDS, 8, 128),
    "rx": (ROUNDS, 2, 32, 128), "ry": (ROUNDS, 2, 16, 128), "rz": (ROUNDS, 2, 8, 128), "mz": (8, 128),
    "sum": (256, 128), "rep": (10 * 48, 128),
    "k1": (18, 32, 128), "f1": (18, 32, 128), "u1a": (18, 32, 128), "u1b": (18, 32, 128),
    "w1": (6, 18, 32, 128), "d1": (18, 32, 128), "i1": (18, 32, 128),
    "zp1": (2, 16, 128), "zb1": (2, 2, 3, 32, 128),
    "k2": (16, 24, 128), "f2": (16, 24, 128), "u2a": (16, 24, 128), "u2b": (16, 24, 128),
    "w2": (6, 16, 24, 128), "d2": (16, 24, 128), "i2": (16, 24, 128),
    "p2": (2, 2, 8, 128), "r2": (2, 27, 2, 8, 128),
    "k3": (22, 24, 128), "f3": (22, 24, 128), "u3a": (22, 24, 128), "u3b": (22, 24, 128),
    "w3": (6, 22, 24, 128), "d3": (22, 24, 128), "i3": (22, 24, 128),
    "s3": (2, 6, 8, 128), "r3": (2, 5, 3, 6, 8, 128),
}
COPIES = ROUNDS * 6 + 2 * (26 + 26 + 14)


def lanes(shape):
    return lax.broadcasted_iota(jnp.int32, shape, len(shape) - 1)


def loop(low, high, body):
    def step(i, carry):
        body(i)
        return carry
    lax.fori_loop(low, high, step, 0, unroll=True)


def dot(a, b):
    return jnp.dot(a, b, precision=lax.Precision.HIGHEST, preferred_element_type=F32)


def pool_matrix(split):
    row = lax.broadcasted_iota(jnp.int32, (128, 128), 0)
    col = lax.broadcasted_iota(jnp.int32, (128, 128), 1)
    target = jnp.where(row < split, row // 2, 64 + row // 2)
    return jnp.where(target == col, 0.125, 0.0).astype(F32)


def repeat_matrix(split):
    row = lax.broadcasted_iota(jnp.int32, (128, 128), 0)
    col = lax.broadcasted_iota(jnp.int32, (128, 128), 1)
    origin = jnp.where(col < split, col // 2, 64 + col // 2)
    return jnp.where(origin == row, 1.0, 0.0).astype(F32)


def edge_matrix():
    row = lax.broadcasted_iota(jnp.int32, (128, 128), 0)
    col = lax.broadcasted_iota(jnp.int32, (128, 128), 1)
    hit = ((row == 127) & (col == 0)) | ((row == 64) & (col == 127))
    return jnp.where(hit, 1.0, 0.0).astype(F32)


def kernel(rhs, kap, pressure, residual, *refs):
    s = dict(zip(SCRATCH, refs))
    send, recv = refs[len(SCRATCH):]
    gx, gy, gz = lax.axis_index("gx"), lax.axis_index("gy"), lax.axis_index("gz")

    def device(o):
        return (lax.rem(gx + (o[0] + GX), GX), lax.rem(gy + (o[1] + GY), GY), lax.rem(gz + (o[2] + GZ), GZ))

    def copy(src, dst, o, index):
        return pltpu.make_async_remote_copy(
            src_ref=src, dst_ref=dst, send_sem=send.at[index], recv_sem=recv.at[index],
            device_id=device(o), device_id_type=MESH)

    barrier = pltpu.get_barrier_semaphore()
    for o in PARTNERS:
        pl.semaphore_signal(barrier, inc=1, device_id=device(o), device_id_type=MESH)

    lane8 = lanes((8, 128))
    lane32 = lanes((32, 128))
    total = s["sum"]

    def faces(u, r):
        for x in range(16):
            s["ys"][r, 0, x:x + 1, :] = u[1 + x, 8:9, :]
            s["ys"][r, 1, x:x + 1, :] = u[1 + x, 39:40, :]
        packed = jnp.zeros((8, 128), F32)
        for x in range(16):
            for t in range(4):
                k = 4 * x + t
                moved = pltpu.roll(u[1 + x, 8 + 8 * t:16 + 8 * t, :], (2 * k + 1) % 128, 1)
                packed = jnp.where((lane8 >> 1) == k, moved, packed)
        s["zs"][r] = packed
        base = 6 * r
        copies = []
        for i, o in enumerate(FACES):
            low = i % 2 == 0
            side = 1 if low else 0
            if i < 2:
                src, dst = u.at[1 if low else 16, pl.ds(8, 32)], s["rx"].at[r, side]
            elif i < 4:
                src, dst = s["ys"].at[r, 0 if low else 1], s["ry"].at[r, side]
            else:
                src, dst = s["zs"].at[r], s["rz"].at[r, side]
            copies.append(copy(src, dst, o, base + i))
        for c in copies:
            c.start()
        return copies

    def land(copies, u, r):
        for c in copies:
            c.wait()
        u[0, 8:40, :] = jnp.where(gx > 0, s["rx"][r, 0], 0.0)
        u[17, 8:40, :] = jnp.where(gx < GX - 1, s["rx"][r, 1], 0.0)
        below = jnp.where(gy > 0, s["ry"][r, 0], 0.0)
        above = jnp.where(gy < GY - 1, s["ry"][r, 1], 0.0)
        for x in range(16):
            u[1 + x, 7:8, :] = below[x:x + 1]
            u[1 + x, 40:41, :] = above[x:x + 1]
        left = jnp.where(gz > 0, s["rz"][r, 0], 0.0)
        right = jnp.where(gz < GZ - 1, s["rz"][r, 1], 0.0)
        s["mz"][...] = jnp.where((lane8 & 1) == 0, left, pltpu.roll(right, 126, 1))

    def ends(x):
        packed = s["mz"][...]
        return jnp.concatenate(
            [pltpu.roll(packed, lax.rem(256 - 8 * x - 2 * t, 128), 1) for t in range(4)], axis=0)

    def around0(u, x, end):
        c = u[1 + x, 8:40, :]
        return c, [
            u[x, 8:40, :], u[2 + x, 8:40, :], u[1 + x, 7:39, :], u[1 + x, 9:41, :],
            jnp.where(lane32 == 0, end, pltpu.roll(c, 1, 1)),
            jnp.where(lane32 == 127, end, pltpu.roll(c, 127, 1))]

    def left0(u, x, end):
        c, others = around0(u, x, end)
        acc = rhs[x] - s["d0"][x] * c
        for i in range(6):
            acc = acc + s["w0"][i, x] * others[i]
        return c, acc

    def inside(lv, p):
        n, level = lv["n"], lv["level"]
        shape = (lv["rows"], 128)
        lane = lanes(shape)
        row = lax.broadcasted_iota(jnp.int32, shape, 0)
        x = gx * n[0] + (p - lv["px"])
        y = gy * n[1] + (row - lv["py"])
        z = gz * n[2] + jnp.where(lane < lv["right"], lane, lane - 128)
        ok = (lane < lv["right"]) | (lane >= lv["left"])
        ok = ok & (y >= 0) & (y < 256 >> level) & (z >= 0) & (z < 512 >> level)
        return ok & (x >= 0) & (x < 256 >> level)

    def around(u, p, rows):
        c = u[p]
        return c, [u[p - 1], u[p + 1], pltpu.roll(c, 1, 0), pltpu.roll(c, rows - 1, 0),
                   pltpu.roll(c, 1, 1), pltpu.roll(c, 127, 1)]

    def weights(lv, k, w, d, inv):
        scale = 0.5 * 0.25 ** lv["level"]

        def clear(p):
            k[p] = jnp.where(inside(lv, p), k[p], 0.0)

        row = lax.broadcasted_iota(jnp.int32, (lv["rows"], 128), 0)
        ends_y = {2: row == 0, 3: row == lv["rows"] - 1}

        def plane(p):
            c, others = around(k, p, lv["rows"])
            diag = None
            for i in range(6):
                other = jnp.where(ends_y[i], 0.0, others[i]) if i in ends_y else others[i]
                weight = scale * (c + other)
                w[i, p] = jnp.where(ends_y[i], 0.0, weight) if i in ends_y else weight
                diag = weight if diag is None else diag + weight
            d[p] = diag
            inv[p] = jnp.where(inside(lv, p), OMEGA / diag, 0.0)
        loop(0, lv["planes"], clear)
        loop(1, lv["planes"] - 1, plane)

    def rest(lv, u, f, w, d, p):
        c, others = around(u, p, lv["rows"])
        acc = f[p] - d[p] * c
        for i in range(6):
            acc = acc + w[i, p] * others[i]
        return c, acc

    def sweep(lv, u, v, f, w, d, inv, low, high):
        def plane(p):
            c, acc = rest(lv, u, f, w, d, p)
            v[p] = c + inv[p] * acc
        loop(low, high, plane)

    def first(u, f, inv, low, high):
        def plane(p):
            u[p] = f[p] * inv[p]
        loop(low, high, plane)

    def pooled_rows(count, rows, start, keep):
        parts = []
        for i in range(count):
            parts.append(total[pl.ds(rows * i + start, keep, stride=2), :]
                         + total[pl.ds(rows * i + start + 1, keep, stride=2), :])
        return jnp.concatenate(parts, axis=0)

    def sums(count, rows, plane):
        for i in range(count):
            total[rows * i:rows * i + rows, :] = plane(2 * i) + plane(2 * i + 1)

    def to_level1(plane, out, slot):
        sums(8, 32, plane)
        mean = dot(pooled_rows(8, 32, 0, 16), pool_matrix(128))
        for i in range(8):
            out[5 + i, 8:24, :] = mean[16 * i:16 * i + 16]
        lane16 = lanes((16, 128))
        packed = jnp.zeros((16, 128), F32)
        for i in range(8):
            v = mean[16 * i:16 * i + 16]
            packed = jnp.where((lane16 >= 16 * i) & (lane16 < 16 * i + 8), pltpu.roll(v, 16 * i, 1) if i else v, packed)
            packed = jnp.where((lane16 >= 16 * i + 8) & (lane16 < 16 * i + 16),
                               pltpu.roll(v, (16 * i + 8 - 56) % 128, 1), packed)
        s["zp1"][slot] = packed

    def send1(out, slot, base):
        copies = []
        for i, (a, b, c) in enumerate(NEAR):
            rows_src = {-1: (8, 8), 0: (8, 16), 1: (16, 8)}[b]
            rows_dst = {-1: 24, 0: 8, 1: 0}[b]
            if c == 0:
                first_plane, count, to = {-1: (5, 5, 13), 0: (5, 8, 5), 1: (8, 5, 0)}[a]
                src = out.at[pl.ds(first_plane, count), pl.ds(rows_src[0], rows_src[1])]
                dst = out.at[pl.ds(to, count), pl.ds(rows_dst, rows_src[1])]
            else:
                src = s["zp1"].at[slot, pl.ds(rows_src[0] - 8, rows_src[1])]
                dst = s["zb1"].at[slot, 0 if c == 1 else 1, 1 - a, pl.ds(rows_dst, rows_src[1])]
            copies.append(copy(src, dst, (a, b, c), base + i))
        for c in copies:
            c.start()
        return copies

    def land1(copies, out, slot):
        for c in copies:
            c.wait()
        for p in range(18):
            x = p - 5
            a = -1 if x < 0 else (0 if x < 8 else 1)
            q = x - 8 * a
            low = pltpu.roll(s["zb1"][slot, 0, a + 1], (120 - 16 * q - 8) % 128, 1)
            high = pltpu.roll(s["zb1"][slot, 1, a + 1], (64 - 16 * q) % 128, 1)
            out[p] = jnp.where(lane32 < 64, out[p],
                               jnp.where(lane32 < 72, high, jnp.where(lane32 >= 120, low, 0.0)))

    def to_level2(plane, first_q, count, slot):
        sums(count, 32, plane)
        rows = pooled_rows(count, 32, 8, 8)
        rows = jnp.where(lanes(rows.shape) < 64, rows, 0.0)
        mean = dot(rows, pool_matrix(128))
        packs = [jnp.zeros((8, 128), F32), jnp.zeros((8, 128), F32)]
        for i in range(count):
            q = first_q + i
            v = mean[8 * i:8 * i + 8]
            packs[q // 4] = packs[q // 4] + (pltpu.roll(v, 32 * (q % 4), 1) if q % 4 else v)
        s["p2"][slot, 0] = packs[0]
        s["p2"][slot, 1] = packs[1]

    def slot2(a, b, c):
        return 9 * (a + 1) + 3 * (b + 1) + (c + 1)

    def send2(slot, base):
        copies = []
        for i, o in enumerate(NEAR):
            copies.append(copy(s["p2"].at[slot], s["r2"].at[slot, slot2(-o[0], -o[1], -o[2])], o, base + i))
        for c in copies:
            c.start()
        s["r2"][slot, slot2(0, 0, 0)] = s["p2"][slot]
        return copies

    def land2(copies, out, slot):
        for c in copies:
            c.wait()
        for p in range(16):
            x = p - 6
            a = -1 if x < 0 else (0 if x < 4 else 1)
            q = x - 4 * a + 2

            def part(b, c, place):
                v = s["r2"][slot, slot2(a, b, c), q // 4]
                shift = (place - 32 * (q % 4)) % 128
                return pltpu.roll(v, shift, 1) if shift else v
            for b in (-1, 0, 1):
                out[p, 8 * (b + 1):8 * (b + 2), :] = jnp.where(
                    lane8 < 32, part(b, 0, 0),
                    jnp.where(lane8 < 64, part(b, 1, 32), jnp.where(lane8 >= 96, part(b, -1, 96), 0.0)))

    def to_level3(plane, slot):
        for i in range(6):
            v = plane(2 * i) + plane(2 * i + 1)
            total[40 * i:40 * i + 24, :] = v
            total[40 * i + 24:40 * i + 32, :] = v[:8]
            total[40 * i + 32:40 * i + 40, :] = v[:8]
        rows = jnp.concatenate([pooled_rows(6, 40, 4, 8), pooled_rows(6, 40, 20, 8)], axis=0)
        mean = dot(rows, pool_matrix(64))
        for i in range(6):
            more = pltpu.roll(mean[48 + 8 * i:56 + 8 * i], 48, 1)
            s["s3"][slot, i] = jnp.where((lane8 >= 32) & (lane8 < 80), more, mean[8 * i:8 * i + 8])

    def send3(slot, base):
        copies = []
        for i, (a, b, c) in enumerate(FAR):
            start, count = {0: (0, 6), 2: (0, 5), -2: (1, 5), 4: (0, 5), -4: (1, 5)}[a]
            if slot == 1 and abs(a) == 4:
                start, count = 1, 4
            copies.append(copy(
                s["s3"].at[slot, pl.ds(start, count)],
                s["r3"].at[slot, 2 - a // 2, 1 - b // 2, pl.ds(start, count)], (a, b, c), base + i))
        for c in copies:
            c.start()
        s["r3"][slot, 2, 1] = s["s3"][slot]
        return copies

    def land3(copies, out, slot, low, high):
        for c in copies:
            c.wait()
        row8 = lax.broadcasted_iota(jnp.int32, (8, 128), 0)
        edge = {-1: (gy < 2) & (row8 >= 6), 1: (gy >= GY - 2) & (row8 < 2)}
        others = {-6: (-2, gx < 4), -2: (0, gx < 2), 3: (0, gx >= GX - 2), 7: (2, gx >= GX - 4)}
        for p in range(low, high):
            x = p - 10
            a = -4 if x < -5 else -2 if x < -1 else 0 if x < 3 else 2 if x < 7 else 4

            def part(b):
                v = s["r3"][slot, 2 + a // 2, 1 + b, x - 2 * a + 2]
                if x in others:
                    near, when = others[x]
                    v = jnp.where(when, s["r3"][slot, 2 + near // 2, 1 + b, x - 2 * near + 2], v)
                return v
            middle = part(0)
            more = pltpu.roll(middle, 80, 1)
            out[p, 0:8, :] = jnp.where(edge[-1], more, part(-1))
            out[p, 8:16, :] = middle
            out[p, 16:24, :] = jnp.where(edge[1], more, part(1))

    def repeat_rows(value, count, rows, start, keep):
        rep = s["rep"]
        for i in range(count):
            v = value[rows * i + start:rows * i + start + keep]
            rep[pl.ds(2 * keep * i, keep, stride=2), :] = v
            rep[pl.ds(2 * keep * i + 1, keep, stride=2), :] = v

    for x in range(16):
        s["k0"][1 + x, 8:40, :] = kap[x]
    to_level1(lambda x: kap[x], s["k1"], 0)
    base1, base2, base3 = 6 * ROUNDS, 6 * ROUNDS + 52, 6 * ROUNDS + 104

    pl.semaphore_wait(barrier, len(PARTNERS))

    moving0 = faces(s["k0"], 0)
    moving1 = send1(s["k1"], 0, base1)
    land(moving0, s["k0"], 0)

    def weights0(x):
        c, others = around0(s["k0"], x, ends(x))
        diag = None
        for i in range(6):
            weight = 0.5 * (c + others[i])
            s["w0"][i, x] = weight
            diag = weight if diag is None else diag + weight
        s["d0"][x] = diag
        inv = OMEGA / diag
        s["i0"][x] = inv
        s["ua"][1 + x, 8:40, :] = rhs[x] * inv
    loop(0, 16, weights0)

    moving0 = faces(s["ua"], 1)
    land1(moving1, s["k1"], 0)
    to_level2(lambda i: s["k1"][1 + i], 0, 8, 0)
    moving2 = send2(0, base2)
    land(moving0, s["ua"], 1)

    def sweep0(src, out):
        def plane(x):
            c, acc = left0(src, x, ends(x))
            out[1 + x, 8:40, :] = c + s["i0"][x] * acc
        loop(0, 16, plane)

    sweep0(s["ua"], s["ub"])
    moving0 = faces(s["ub"], 2)
    land2(moving2, s["k2"], 0)
    to_level3(lambda i: s["k2"][2 + i], 0)
    moving3 = send3(0, base3)
    weights(L1, s["k1"], s["w1"], s["d1"], s["i1"])
    land(moving0, s["ub"], 2)

    def rest0(x):
        residual[x] = left0(s["ub"], x, ends(x))[1]
    loop(0, 16, rest0)
    to_level1(lambda x: residual[x], s["f1"], 1)
    moving1 = send1(s["f1"], 1, base1 + 26)
    weights(L2, s["k2"], s["w2"], s["d2"], s["i2"])
    land3(moving3, s["k3"], 0, 0, 22)
    land1(moving1, s["f1"], 1)

    first(s["u1a"], s["f1"], s["i1"], 1, 17)
    sweep(L1, s["u1a"], s["u1b"], s["f1"], s["w1"], s["d1"], s["i1"], 2, 16)

    def rest1(p):
        s["u1a"][p] = rest(L1, s["u1b"], s["f1"], s["w1"], s["d1"], p)[1]
    loop(3, 15, rest1)
    to_level2(lambda i: s["u1a"][3 + i], 1, 6, 1)
    moving2 = send2(1, base2 + 26)
    weights(L3, s["k3"], s["w3"], s["d3"], s["i3"])
    land2(moving2, s["f2"], 1)

    first(s["u2a"], s["f2"], s["i2"], 1, 15)
    sweep(L2, s["u2a"], s["u2b"], s["f2"], s["w2"], s["d2"], s["i2"], 2, 14)

    def rest2(p):
        s["u2a"][p] = rest(L2, s["u2b"], s["f2"], s["w2"], s["d2"], p)[1]
    s["u2b"][1] = jnp.zeros((24, 128), F32)
    s["u2b"][14] = jnp.zeros((24, 128), F32)
    loop(2, 14, rest2)
    to_level3(lambda i: s["u2a"][2 + i], 1)
    land3(send3(1, base3 + 14), s["f3"], 1, 1, 21)

    u, v = s["u3a"], s["u3b"]
    first(u, s["f3"], s["i3"], 1, 21)
    for step in range(COARSE_SWEEPS - 1):
        sweep(L3, u, v, s["f3"], s["w3"], s["d3"], s["i3"], 2 + step, 20 - step)
        u, v = v, u

    rep = s["rep"]
    value = dot(u[8:14].reshape(6 * 24, 128), repeat_matrix(64))
    repeat_rows(value, 6, 24, 6, 12)
    for p in range(2, 14):
        i = p // 2 - 1
        s["u2b"][p] = s["u2b"][p] + rep[24 * i:24 * i + 24, :]
    sweep(L2, s["u2b"], s["u2a"], s["f2"], s["w2"], s["d2"], s["i2"], 3, 13)
    sweep(L2, s["u2a"], s["u2b"], s["f2"], s["w2"], s["d2"], s["i2"], 4, 12)

    value = dot(s["u2b"][4:12].reshape(8 * 24, 128), repeat_matrix(96))
    repeat_rows(value, 8, 24, 4, 16)
    for p in range(2, 16):
        i = (p + 7) // 2 - 4
        s["u1b"][p] = s["u1b"][p] + rep[32 * i:32 * i + 32, :]
    sweep(L1, s["u1b"], s["u1a"], s["f1"], s["w1"], s["d1"], s["i1"], 3, 15)
    sweep(L1, s["u1a"], s["u1b"], s["f1"], s["w1"], s["d1"], s["i1"], 4, 14)

    value = s["u1b"][4:14].reshape(10 * 32, 128)
    repeat_rows(dot(value, edge_matrix()), 10, 32, 4, 24)
    for x in range(16):
        i = (x + 10) // 2 - 4
        s["h0"][x] = ends(x) + rep[48 * i + 8:48 * i + 40, :]
    repeat_rows(dot(value, repeat_matrix(128)), 10, 32, 4, 24)
    for p in range(18):
        i = (p + 9) // 2 - 4
        if p in (0, 17):
            s["ub"][p, 8:40, :] = s["ub"][p, 8:40, :] + rep[48 * i + 8:48 * i + 40, :]
        else:
            s["ub"][p, 7:41, :] = s["ub"][p, 7:41, :] + rep[48 * i + 7:48 * i + 41, :]

    def up0(x):
        c, acc = left0(s["ub"], x, s["h0"][x])
        s["ua"][1 + x, 8:40, :] = c + s["i0"][x] * acc
    loop(0, 16, up0)
    land(faces(s["ua"], 3), s["ua"], 3)
    sweep0(s["ua"], s["ub"])
    moving0 = faces(s["ub"], 4)
    for x in range(16):
        pressure[x] = s["ub"][1 + x, 8:40, :]
    land(moving0, s["ub"], 4)

    def end0(x):
        residual[x] = left0(s["ub"], x, ends(x))[1]
    loop(0, 16, end0)


def cycle(rhs, kappa):
    block = jax.ShapeDtypeStruct((16, 32, 128), F32)
    vmem = pl.BlockSpec(memory_space=pltpu.VMEM)
    return pl.pallas_call(
        kernel,
        out_shape=(block, block),
        in_specs=[vmem, vmem],
        out_specs=(vmem, vmem),
        scratch_shapes=[pltpu.VMEM(shape, F32) for shape in SCRATCH.values()] + [
            pltpu.SemaphoreType.DMA((COPIES,)), pltpu.SemaphoreType.DMA((COPIES,))],
        compiler_params=pltpu.CompilerParams(
            collective_id=0, has_side_effects=True, vmem_limit_bytes=40 * 1024 * 1024),
        cost_estimate=pl.CostEstimate(flops=40_000_000, bytes_accessed=1_048_576, transcendentals=0),
    )(rhs, kappa)


def solution(mesh):
    placed = (P("gx", "gy", "gz"), P("gx", "gy", "gz"))
    return jax.shard_map(
        cycle, mesh=mesh, in_specs=placed, out_specs=(P("gx", "gy", "gz"), P("gx", "gy", "gz")), check_vma=False)
```

time: 661 us -> 76.5 us (0.12)
  starting transfers between devices: 371 us -> 0 us
  waiting for transfers between devices: 207 us -> 0 us
  Pallas kernels: 0 us -> 72.3 us
  local copies, waits for them, and re-layouts: 49.7 us -> 3.3 us
  other arithmetic: 25 us -> 0 us
    ppermute x144 -> x0, starting transfers between devices: 371 us -> none  [the longest x72 256 us: with_halo(): lax.ppermute(tail, axis, [(i, (i + 1) % count) for i in range(ends)])]
    ppermute x144 -> x0, waiting for transfers between devices: 207 us -> none  [the longest x72 181 us: with_halo(): lax.ppermute(head, axis, [((i + 1) % count, i) for i in range(ends)])]
    pallas_call x0 -> x1, Pallas kernels: none -> 72.3 us  [cycle(): pl.pallas_call(kernel, out_shape=(block, block), in_specs=[vmem, vmem], o...]
    reshape x10 -> x0, local copies, waits for them, and re-layouts: 41.7 us -> none  [the longest x4 40.6 us: restrict(): return field.reshape(a // 2, 2, b // 2, 2, c // 2, 2).mean(axis=(1, 3, 5))]
    reduce_sum x6 -> x0, other arithmetic: 17.8 us -> none  [restrict(): return field.reshape(a // 2, 2, b // 2, 2, c // 2, 2).mean(axis=(1, 3, 5))]
  transfers between devices with their start and end apart: 144 -> 0, of which waited for: 64 -> 0; matrix products, arithmetic and copies ran while one was open for 9% -> 0% of each run, Pallas kernels for 0% -> 0%
where the time goes in v1:
time: 76.5 us; the launch traced here: 76.3 us
  Pallas kernels  72.3 us (95%)
  local copies, waits for them, and re-layouts  3.3 us (4%)
    pallas_call x1, Pallas kernels, cycle(): pl.pallas_call(kernel, out_shape=(block, block), in_specs=[vmem, vmem], o...  72.3 us
    unnamed x6, local copies, waits for them, and re-layouts  3.3 us

profile of v1, /device:TPU:1, one launch (start us, length us, event | category | flops | bytes accessed | tf_op | source)
XLA Modules:
  0.0 76.3 jit_solution(1606815825985655316)
XLA Ops:
  0.6 0.0 copy-start
  0.6 0.9 %copy-done = f32[16,32,128]{2,1,0:T(8,128)S(1)} copy-done((f32[16,32,128]{2,1,0:T(8,128)S(1)}, f32[16,32,128]{2,1,0:T(8,128)}, u32[]{:S(2)}) %copy-start) | copy-done | bytes 262168
  1.6 0.0 copy-start.1
  1.6 0.9 %copy-done.1 = f32[16,32,128]{2,1,0:T(8,128)S(1)} copy-done((f32[16,32,128]{2,1,0:T(8,128)S(1)}, f32[16,32,128]{2,1,0:T(8,128)}, u32[]{:S(2)}) %copy-start.1) | copy-done | bytes 262168
  2.5 72.3 %shard_map.41 = (f32[16,32,128]{2,1,0:T(8,128)S(1)}, f32[16,32,128]{2,1,0:T(8,128)S(1)}) custom-call(f32[16,32,128]{2,1,0:T(8,128)S(1)} %copy-done, f32[16,32,128]{2,1,0:T(8,128)S(1)} %copy-done.1), custom_call_target="tpu_custom_call" | custom-call | flops 40000000 | bytes 1048576 | tf_op jit(solution)/shard_map/pallas_call | solution.py:500
  74.9 0.7 copy.6
  75.6 0.7 copy.7
Async XLA Ops:
  0.6 1.0 %copy-start = (f32[16,32,128]{2,1,0:T(8,128)S(1)}, f32[16,32,128]{2,1,0:T(8,128)}, u32[]{:S(2)}) copy-start(f32[16,32,128]{2,1,0:T(8,128)} %rhs.1) | copy-start | bytes 786436
  1.6 0.9 %copy-start.1 = (f32[16,32,128]{2,1,0:T(8,128)S(1)}, f32[16,32,128]{2,1,0:T(8,128)}, u32[]{:S(2)}) copy-start(f32[16,32,128]{2,1,0:T(8,128)} %kap.1) | copy-start | bytes 786436

commit v2 on v1

--- a/solution.py
+++ b/solution.py
@@ -14,9 +14,9 @@
 COARSE_SWEEPS = 8
 GX, GY, GZ = 16, 8, 4
 FACES = [(-1, 0, 0), (1, 0, 0), (0, -1, 0), (0, 1, 0), (0, 0, -1), (0, 0, 1)]
-NEAR = [o for o in itertools.product((-1, 0, 1), repeat=3) if o != (0, 0, 0)]
-FAR = [(a, b, 0) for a in (-4, -2, 0, 2, 4) for b in (-2, 0, 2) if (a, b) != (0, 0)]
-PARTNERS = NEAR + FAR
+NEAR = sorted((o for o in itertools.product((-1, 0, 1), repeat=3) if o != (0, 0, 0)), key=lambda o: -sum(map(abs, o)))
+FAR = sorted(((a, b, 0) for a in (-4, -2, 0, 2, 4) for b in (-2, 0, 2) if (a, b) != (0, 0)),
+             key=lambda o: -sum(map(abs, o)))
 ROUNDS = 5
 
 L1 = dict(planes=18, rows=32, px=5, py=8, n=(8, 16, 64), right=72, left=120, level=1)
@@ -25,7 +25,7 @@
 
 SCRATCH = {
     "ua": (18, 48, 128), "ub": (18, 48, 128), "k0": (18, 48, 128),
-    "w0": (6, 16, 32, 128), "d0": (16, 32, 128), "i0": (16, 32, 128), "h0": (16, 32, 128),
+    "f0": (16, 32, 128), "w0": (6, 16, 32, 128), "d0": (16, 32, 128), "i0": (16, 32, 128), "h0": (16, 32, 128),
     "ys": (ROUNDS, 2, 16, 128), "zs": (ROUNDS, 8, 128),
     "rx": (ROUNDS, 2, 32, 128), "ry": (ROUNDS, 2, 16, 128), "rz": (ROUNDS, 2, 8, 128), "mz": (8, 128),
     "sum": (256, 128), "rep": (10 * 48, 128),
@@ -78,9 +78,10 @@
     return jnp.where(hit, 1.0, 0.0).astype(F32)
 
 
-def kernel(rhs, kap, pressure, residual, *refs):
+def kernel(rhs_in, kap_in, pressure, residual, *refs):
     s = dict(zip(SCRATCH, refs))
-    send, recv = refs[len(SCRATCH):]
+    send, recv, load = refs[len(SCRATCH):]
+    rhs = s["f0"]
     gx, gy, gz = lax.axis_index("gx"), lax.axis_index("gy"), lax.axis_index("gz")
 
     def device(o):
@@ -92,8 +93,12 @@
             device_id=device(o), device_id_type=MESH)
 
     barrier = pltpu.get_barrier_semaphore()
-    for o in PARTNERS:
+    for o in FACES:
         pl.semaphore_signal(barrier, inc=1, device_id=device(o), device_id_type=MESH)
+    load_kap = pltpu.make_async_copy(kap_in, s["k0"].at[pl.ds(1, 16), pl.ds(8, 32)], load.at[0])
+    load_rhs = pltpu.make_async_copy(rhs_in, rhs, load.at[1])
+    load_kap.start()
+    load_rhs.start()
 
     lane8 = lanes((8, 128))
     lane32 = lanes((32, 128))
@@ -367,15 +372,12 @@
             rep[pl.ds(2 * keep * i, keep, stride=2), :] = v
             rep[pl.ds(2 * keep * i + 1, keep, stride=2), :] = v
 
-    for x in range(16):
-        s["k0"][1 + x, 8:40, :] = kap[x]
-    to_level1(lambda x: kap[x], s["k1"], 0)
     base1, base2, base3 = 6 * ROUNDS, 6 * ROUNDS + 52, 6 * ROUNDS + 104
-
-    pl.semaphore_wait(barrier, len(PARTNERS))
-
+    load_kap.wait()
+    pl.semaphore_wait(barrier, len(FACES))
     moving0 = faces(s["k0"], 0)
-    moving1 = send1(s["k1"], 0, base1)
+    to_level1(lambda x: s["k0"][1 + x, 8:40, :], s["k1"], 0)
+    load_rhs.wait()
     land(moving0, s["k0"], 0)
 
     def weights0(x):
@@ -392,9 +394,6 @@
     loop(0, 16, weights0)
 
     moving0 = faces(s["ua"], 1)
-    land1(moving1, s["k1"], 0)
-    to_level2(lambda i: s["k1"][1 + i], 0, 8, 0)
-    moving2 = send2(0, base2)
     land(moving0, s["ua"], 1)
 
     def sweep0(src, out):
@@ -405,10 +404,7 @@
 
     sweep0(s["ua"], s["ub"])
     moving0 = faces(s["ub"], 2)
-    land2(moving2, s["k2"], 0)
-    to_level3(lambda i: s["k2"][2 + i], 0)
-    moving3 = send3(0, base3)
-    weights(L1, s["k1"], s["w1"], s["d1"], s["i1"])
+    coefficient1 = send1(s["k1"], 0, base1)
     land(moving0, s["ub"], 2)
 
     def rest0(x):
@@ -416,8 +412,10 @@
     loop(0, 16, rest0)
     to_level1(lambda x: residual[x], s["f1"], 1)
     moving1 = send1(s["f1"], 1, base1 + 26)
-    weights(L2, s["k2"], s["w2"], s["d2"], s["i2"])
-    land3(moving3, s["k3"], 0, 0, 22)
+    land1(coefficient1, s["k1"], 0)
+    to_level2(lambda i: s["k1"][1 + i], 0, 8, 0)
+    coefficient2 = send2(0, base2)
+    weights(L1, s["k1"], s["w1"], s["d1"], s["i1"])
     land1(moving1, s["f1"], 1)
 
     first(s["u1a"], s["f1"], s["i1"], 1, 17)
@@ -428,7 +426,10 @@
     loop(3, 15, rest1)
     to_level2(lambda i: s["u1a"][3 + i], 1, 6, 1)
     moving2 = send2(1, base2 + 26)
-    weights(L3, s["k3"], s["w3"], s["d3"], s["i3"])
+    land2(coefficient2, s["k2"], 0)
+    to_level3(lambda i: s["k2"][2 + i], 0)
+    coefficient3 = send3(0, base3)
+    weights(L2, s["k2"], s["w2"], s["d2"], s["i2"])
     land2(moving2, s["f2"], 1)
 
     first(s["u2a"], s["f2"], s["i2"], 1, 15)
@@ -440,7 +441,10 @@
     s["u2b"][14] = jnp.zeros((24, 128), F32)
     loop(2, 14, rest2)
     to_level3(lambda i: s["u2a"][2 + i], 1)
-    land3(send3(1, base3 + 14), s["f3"], 1, 1, 21)
+    moving3 = send3(1, base3 + 14)
+    land3(coefficient3, s["k3"], 0, 0, 22)
+    weights(L3, s["k3"], s["w3"], s["d3"], s["i3"])
+    land3(moving3, s["f3"], 1, 1, 21)
 
     u, v = s["u3a"], s["u3b"]
     first(u, s["f3"], s["i3"], 1, 21)
@@ -500,10 +504,11 @@
     return pl.pallas_call(
         kernel,
         out_shape=(block, block),
-        in_specs=[vmem, vmem],
+        in_specs=[pl.BlockSpec(memory_space=pltpu.HBM)] * 2,
         out_specs=(vmem, vmem),
         scratch_shapes=[pltpu.VMEM(shape, F32) for shape in SCRATCH.values()] + [
-            pltpu.SemaphoreType.DMA((COPIES,)), pltpu.SemaphoreType.DMA((COPIES,))],
+            pltpu.SemaphoreType.DMA((COPIES,)), pltpu.SemaphoreType.DMA((COPIES,)),
+            pltpu.SemaphoreType.DMA((2,))],
         compiler_params=pltpu.CompilerParams(
             collective_id=0, has_side_effects=True, vmem_limit_bytes=40 * 1024 * 1024),
         cost_estimate=pl.CostEstimate(flops=40_000_000, bytes_accessed=1_048_576, transcendentals=0),

time: 76.5 us -> 67.8 us (0.89)
  Pallas kernels: 72.3 us -> 63.7 us
    pallas_call x1, Pallas kernels: 72.3 us -> 63.7 us  [cycle(): pl.pallas_call(kernel, out_shape=(block, block), in_specs=[pl.BlockSpec(m...]
where the time goes in v2:
time: 67.8 us; the launch traced here: 67.6 us
  Pallas kernels  63.7 us (94%)
  local copies, waits for them, and re-layouts  3.3 us (5%)
    pallas_call x1, Pallas kernels, cycle(): pl.pallas_call(kernel, out_shape=(block, block), in_specs=[pl.BlockSpec(m...  63.7 us
    unnamed x6, local copies, waits for them, and re-layouts  3.3 us

profile of v2, /device:TPU:1, one launch (start us, length us, event | category | flops | bytes accessed | tf_op | source)
XLA Modules:
  0.0 67.6 jit_solution(3965578792038138800)
XLA Ops:
  0.6 0.0 copy-start
  0.6 0.9 %copy-done = f32[16,32,128]{2,1,0:T(8,128)S(1)} copy-done((f32[16,32,128]{2,1,0:T(8,128)S(1)}, f32[16,32,128]{2,1,0:T(8,128)}, u32[]{:S(2)}) %copy-start) | copy-done | bytes 262168
  1.6 0.0 copy-start.1
  1.6 0.9 %copy-done.1 = f32[16,32,128]{2,1,0:T(8,128)S(1)} copy-done((f32[16,32,128]{2,1,0:T(8,128)S(1)}, f32[16,32,128]{2,1,0:T(8,128)}, u32[]{:S(2)}) %copy-start.1) | copy-done | bytes 262168
  2.5 63.7 %shard_map.41 = (f32[16,32,128]{2,1,0:T(8,128)S(1)}, f32[16,32,128]{2,1,0:T(8,128)S(1)}) custom-call(f32[16,32,128]{2,1,0:T(8,128)S(1)} %copy-done, f32[16,32,128]{2,1,0:T(8,128)S(1)} %copy-done.1), custom_call_target="tpu_custom_call" | custom-call | flops 40000000 | bytes 1048576 | tf_op jit(solution)/shard_map/pallas_call | solution.py:504
  66.2 0.7 %copy.6 = f32[16,32,128]{2,1,0:T(8,128)} copy(f32[16,32,128]{2,1,0:T(8,128)S(1)} %get-tuple-element.4) | data formatting | bytes 524288
  66.9 0.7 %copy.7 = f32[16,32,128]{2,1,0:T(8,128)} copy(f32[16,32,128]{2,1,0:T(8,128)S(1)} %get-tuple-element.5) | data formatting | bytes 524288
Async XLA Ops:
  0.6 1.0 %copy-start = (f32[16,32,128]{2,1,0:T(8,128)S(1)}, f32[16,32,128]{2,1,0:T(8,128)}, u32[]{:S(2)}) copy-start(f32[16,32,128]{2,1,0:T(8,128)} %rhs_in.1) | copy-start | bytes 786436
  1.6 0.9 %copy-start.1 = (f32[16,32,128]{2,1,0:T(8,128)S(1)}, f32[16,32,128]{2,1,0:T(8,128)}, u32[]{:S(2)}) copy-start(f32[16,32,128]{2,1,0:T(8,128)} %kap_in.1) | copy-start | bytes 786436

commit v3 on v2

--- a/solution.py
+++ b/solution.py
@@ -10,6 +10,7 @@
 
 MESH = pl.DeviceIdType.MESH
 F32 = jnp.float32
+BF16 = jnp.bfloat16
 OMEGA = 0.8
 COARSE_SWEEPS = 8
 GX, GY, GZ = 16, 8, 4
@@ -18,6 +19,7 @@
 FAR = sorted(((a, b, 0) for a in (-4, -2, 0, 2, 4) for b in (-2, 0, 2) if (a, b) != (0, 0)),
              key=lambda o: -sum(map(abs, o)))
 ROUNDS = 5
+PAIRS = [(0, 5), (1, 2), (3, 4)]
 
 L1 = dict(planes=18, rows=32, px=5, py=8, n=(8, 16, 64), right=72, left=120, level=1)
 L2 = dict(planes=16, rows=24, px=6, py=8, n=(4, 8, 32), right=64, left=96, level=2)
@@ -25,9 +27,9 @@
 
 SCRATCH = {
     "ua": (18, 48, 128), "ub": (18, 48, 128), "k0": (18, 48, 128),
-    "f0": (16, 32, 128), "w0": (6, 16, 32, 128), "d0": (16, 32, 128), "i0": (16, 32, 128), "h0": (16, 32, 128),
+    "f0": (16, 32, 128), "part": (16, 32, 128), "wy": (16, 32, 128), "wz": (16, 32, 128), "w0": (6, 16, 32, 128), "d0": (16, 32, 128), "i0": (16, 32, 128), "h0": (16, 32, 128),
     "ys": (ROUNDS, 2, 16, 128), "zs": (ROUNDS, 8, 128),
-    "rx": (ROUNDS, 2, 32, 128), "ry": (ROUNDS, 2, 16, 128), "rz": (ROUNDS, 2, 8, 128), "mz": (8, 128),
+    "rx": (ROUNDS, 2, 32, 128), "ry": (ROUNDS, 2, 16, 128), "rz": (ROUNDS, 2, 8, 128), "mz": (2, 8, 128),
     "sum": (256, 128), "rep": (10 * 48, 128),
     "k1": (18, 32, 128), "f1": (18, 32, 128), "u1a": (18, 32, 128), "u1b": (18, 32, 128),
     "w1": (6, 18, 32, 128), "d1": (18, 32, 128), "i1": (18, 32, 128),
@@ -37,7 +39,7 @@
     "p2": (2, 2, 8, 128), "r2": (2, 27, 2, 8, 128),
     "k3": (22, 24, 128), "f3": (22, 24, 128), "u3a": (22, 24, 128), "u3b": (22, 24, 128),
     "w3": (6, 22, 24, 128), "d3": (22, 24, 128), "i3": (22, 24, 128),
-    "s3": (2, 6, 8, 128), "r3": (2, 5, 3, 6, 8, 128),
+    "s3": (2, 6, 8, 128), "t3": (2, 3, 8, 128), "r3": (2, 5, 6, 8, 128), "q3": (2, 5, 2, 3, 8, 128),
 }
 COPIES = ROUNDS * 6 + 2 * (26 + 26 + 14)
 
@@ -54,38 +56,44 @@
 
 
 def dot(a, b):
-    return jnp.dot(a, b, precision=lax.Precision.HIGHEST, preferred_element_type=F32)
-
-
-def pool_matrix(split):
+    high = a.astype(BF16)
+    low = (a - high.astype(F32)).astype(BF16)
+    return (jnp.dot(high, b, preferred_element_type=F32) + jnp.dot(low, b, preferred_element_type=F32))
+
+
+def tables():
     row = lax.broadcasted_iota(jnp.int32, (128, 128), 0)
     col = lax.broadcasted_iota(jnp.int32, (128, 128), 1)
-    target = jnp.where(row < split, row // 2, 64 + row // 2)
-    return jnp.where(target == col, 0.125, 0.0).astype(F32)
-
-
-def repeat_matrix(split):
-    row = lax.broadcasted_iota(jnp.int32, (128, 128), 0)
-    col = lax.broadcasted_iota(jnp.int32, (128, 128), 1)
-    origin = jnp.where(col < split, col // 2, 64 + col // 2)
-    return jnp.where(origin == row, 1.0, 0.0).astype(F32)
-
-
-def edge_matrix():
-    row = lax.broadcasted_iota(jnp.int32, (128, 128), 0)
-    col = lax.broadcasted_iota(jnp.int32, (128, 128), 1)
-    hit = ((row == 127) & (col == 0)) | ((row == 64) & (col == 127))
-    return jnp.where(hit, 1.0, 0.0).astype(F32)
+
+    def half(index, split):
+        return jnp.where(index < split, index // 2, 64 + index // 2)
+    pools = [jnp.where(half(row, split) == col, 0.125, 0.0) for split in (128, 64)]
+    repeats = [jnp.where(half(col, split) == row, 1.0, 0.0) for split in (64, 96, 128)]
+    edges = jnp.where(((row == 127) & (col == 0)) | ((row == 64) & (col == 127)), 1.0, 0.0)
+    return [m.astype(BF16) for m in pools + repeats + [edges]]
+
+
+POOL, POOL_HALO, REPEAT_64, REPEAT_96, REPEAT_128, EDGES = range(6)
 
 
 def kernel(rhs_in, kap_in, pressure, residual, *refs):
     s = dict(zip(SCRATCH, refs))
-    send, recv, load = refs[len(SCRATCH):]
+    send, recv, load, tab = refs[len(SCRATCH):]
     rhs = s["f0"]
     gx, gy, gz = lax.axis_index("gx"), lax.axis_index("gy"), lax.axis_index("gz")
 
+    at_x = {a: (gx + a) & (GX - 1) for a in (-4, -2, -1, 1, 2, 4)} | {0: gx}
+    at_y = {a: (gy + a) & (GY - 1) for a in (-2, -1, 1, 2)} | {0: gy}
+    at_z = {a: (gz + a) & (GZ - 1) for a in (-1, 1)} | {0: gz}
+    sent = []
+
     def device(o):
-        return (lax.rem(gx + (o[0] + GX), GX), lax.rem(gy + (o[1] + GY), GY), lax.rem(gz + (o[2] + GZ), GZ))
+        return (at_x[o[0]], at_y[o[1]], at_z[o[2]])
+
+    def drain():
+        for c in sent:
+            c.wait_send()
+        sent.clear()
 
     def copy(src, dst, o, index):
         return pltpu.make_async_remote_copy(
@@ -104,7 +112,7 @@
     lane32 = lanes((32, 128))
     total = s["sum"]
 
-    def faces(u, r):
+    def pack(u, r):
         for x in range(16):
             s["ys"][r, 0, x:x + 1, :] = u[1 + x, 8:9, :]
             s["ys"][r, 1, x:x + 1, :] = u[1 + x, 39:40, :]
@@ -115,6 +123,8 @@
                 moved = pltpu.roll(u[1 + x, 8 + 8 * t:16 + 8 * t, :], (2 * k + 1) % 128, 1)
                 packed = jnp.where((lane8 >> 1) == k, moved, packed)
         s["zs"][r] = packed
+
+    def faces(u, r):
         base = 6 * r
         copies = []
         for i, o in enumerate(FACES):
@@ -129,11 +139,15 @@
             copies.append(copy(src, dst, o, base + i))
         for c in copies:
             c.start()
+        drain()
         return copies
 
-    def land(copies, u, r):
+    def arrive(copies):
         for c in copies:
-            c.wait()
+            c.wait_recv()
+        sent.extend(copies)
+
+    def land(u, r, out):
         u[0, 8:40, :] = jnp.where(gx > 0, s["rx"][r, 0], 0.0)
         u[17, 8:40, :] = jnp.where(gx < GX - 1, s["rx"][r, 1], 0.0)
         below = jnp.where(gy > 0, s["ry"][r, 0], 0.0)
@@ -141,28 +155,51 @@
         for x in range(16):
             u[1 + x, 7:8, :] = below[x:x + 1]
             u[1 + x, 40:41, :] = above[x:x + 1]
+        merge(r, out)
+
+    def merge(r, out):
         left = jnp.where(gz > 0, s["rz"][r, 0], 0.0)
         right = jnp.where(gz < GZ - 1, s["rz"][r, 1], 0.0)
-        s["mz"][...] = jnp.where((lane8 & 1) == 0, left, pltpu.roll(right, 126, 1))
-
-    def ends(x):
-        packed = s["mz"][...]
+        s["mz"][out] = jnp.where((lane8 & 1) == 0, left, pltpu.roll(right, 126, 1))
+
+    def ends(x, at):
+        packed = s["mz"][at]
         return jnp.concatenate(
-            [pltpu.roll(packed, lax.rem(256 - 8 * x - 2 * t, 128), 1) for t in range(4)], axis=0)
-
-    def around0(u, x, end):
+            [pltpu.roll(packed, (-8 * x - 2 * t) % 128, 1) if x + t else packed for t in range(4)], axis=0)
+
+    def around0(u, x):
         c = u[1 + x, 8:40, :]
-        return c, [
-            u[x, 8:40, :], u[2 + x, 8:40, :], u[1 + x, 7:39, :], u[1 + x, 9:41, :],
-            jnp.where(lane32 == 0, end, pltpu.roll(c, 1, 1)),
-            jnp.where(lane32 == 127, end, pltpu.roll(c, 127, 1))]
-
-    def left0(u, x, end):
-        c, others = around0(u, x, end)
+        return c, [u[x, 8:40, :], u[2 + x, 8:40, :], u[1 + x, 7:39, :], u[1 + x, 9:41, :],
+                   pltpu.roll(c, 1, 1), pltpu.roll(c, 127, 1)]
+
+    def core0(u, x):
+        c, others = around0(u, x)
         acc = rhs[x] - s["d0"][x] * c
         for i in range(6):
             acc = acc + s["w0"][i, x] * others[i]
         return c, acc
+
+    def partial0(u):
+        for x in range(16):
+            s["part"][x] = core0(u, x)[1]
+
+    def finish0(r, x):
+        acc = s["part"][x] + s["wz"][x] * ends(x, 0)
+        if x == 0:
+            acc = acc + s["w0"][0, 0] * jnp.where(gx > 0, s["rx"][r, 0], 0.0)
+        if x == 15:
+            acc = acc + s["w0"][1, 15] * jnp.where(gx < GX - 1, s["rx"][r, 1], 0.0)
+        below = jnp.broadcast_to(jnp.where(gy > 0, s["ry"][r, 0, x:x + 1, :], 0.0), (8, 128))
+        above = jnp.broadcast_to(jnp.where(gy < GY - 1, s["ry"][r, 1, x:x + 1, :], 0.0), (8, 128))
+        return jnp.concatenate(
+            [acc[:8] + s["wy"][x, :8] * below, acc[8:24], acc[24:] + s["wy"][x, 24:] * above], axis=0)
+
+    def clear0(u):
+        u[0] = jnp.zeros((48, 128), F32)
+        u[17] = jnp.zeros((48, 128), F32)
+        for x in range(16):
+            u[1 + x, 0:8, :] = jnp.zeros((8, 128), F32)
+            u[1 + x, 40:48, :] = jnp.zeros((8, 128), F32)
 
     def inside(lv, p):
         n, level = lv["n"], lv["level"]
@@ -212,8 +249,11 @@
 
     def sweep(lv, u, v, f, w, d, inv, low, high):
         def plane(p):
-            c, acc = rest(lv, u, f, w, d, p)
-            v[p] = c + inv[p] * acc
+            c, others = around(u, p, lv["rows"])
+            acc = f[p]
+            for i in range(6):
+                acc = acc + w[i, p] * others[i]
+            v[p] = (1.0 - OMEGA) * c + inv[p] * acc
         loop(low, high, plane)
 
     def first(u, f, inv, low, high):
@@ -234,7 +274,7 @@
 
     def to_level1(plane, out, slot):
         sums(8, 32, plane)
-        mean = dot(pooled_rows(8, 32, 0, 16), pool_matrix(128))
+        mean = dot(pooled_rows(8, 32, 0, 16), tab[POOL])
         for i in range(8):
             out[5 + i, 8:24, :] = mean[16 * i:16 * i + 16]
         lane16 = lanes((16, 128))
@@ -252,7 +292,8 @@
             rows_src = {-1: (8, 8), 0: (8, 16), 1: (16, 8)}[b]
             rows_dst = {-1: 24, 0: 8, 1: 0}[b]
             if c == 0:
-                first_plane, count, to = {-1: (5, 5, 13), 0: (5, 8, 5), 1: (8, 5, 0)}[a]
+                deep = 5 - slot
+                first_plane, count, to = {-1: (5, deep, 13), 0: (5, 8, 5), 1: (13 - deep, deep, 5 - deep)}[a]
                 src = out.at[pl.ds(first_plane, count), pl.ds(rows_src[0], rows_src[1])]
                 dst = out.at[pl.ds(to, count), pl.ds(rows_dst, rows_src[1])]
             else:
@@ -264,8 +305,12 @@
         return copies
 
     def land1(copies, out, slot):
-        for c in copies:
-            c.wait()
+        for c, o in zip(copies, NEAR):
+            c.wait_recv()
+            if o[2] == 0:
+                c.wait_send()
+            else:
+                sent.append(c)
         for p in range(18):
             x = p - 5
             a = -1 if x < 0 else (0 if x < 8 else 1)
@@ -279,7 +324,7 @@
         sums(count, 32, plane)
         rows = pooled_rows(count, 32, 8, 8)
         rows = jnp.where(lanes(rows.shape) < 64, rows, 0.0)
-        mean = dot(rows, pool_matrix(128))
+        mean = dot(rows, tab[POOL])
         packs = [jnp.zeros((8, 128), F32), jnp.zeros((8, 128), F32)]
         for i in range(count):
             q = first_q + i
@@ -301,8 +346,7 @@
         return copies
 
     def land2(copies, out, slot):
-        for c in copies:
-            c.wait()
+        arrive(copies)
         for p in range(16):
             x = p - 6
             a = -1 if x < 0 else (0 if x < 4 else 1)
@@ -324,10 +368,14 @@
             total[40 * i + 24:40 * i + 32, :] = v[:8]
             total[40 * i + 32:40 * i + 40, :] = v[:8]
         rows = jnp.concatenate([pooled_rows(6, 40, 4, 8), pooled_rows(6, 40, 20, 8)], axis=0)
-        mean = dot(rows, pool_matrix(64))
+        mean = dot(rows, tab[POOL_HALO])
         for i in range(6):
             more = pltpu.roll(mean[48 + 8 * i:56 + 8 * i], 48, 1)
             s["s3"][slot, i] = jnp.where((lane8 >= 32) & (lane8 < 80), more, mean[8 * i:8 * i + 8])
+
+        for i, (p, q) in enumerate(PAIRS):
+            s["t3"][slot, i] = jnp.where(
+                lane8 < 64, pltpu.roll(s["s3"][slot, p], 16, 1), pltpu.roll(s["s3"][slot, q], 80, 1))
 
     def send3(slot, base):
         copies = []
@@ -335,17 +383,21 @@
             start, count = {0: (0, 6), 2: (0, 5), -2: (1, 5), 4: (0, 5), -4: (1, 5)}[a]
             if slot == 1 and abs(a) == 4:
                 start, count = 1, 4
-            copies.append(copy(
-                s["s3"].at[slot, pl.ds(start, count)],
-                s["r3"].at[slot, 2 - a // 2, 1 - b // 2, pl.ds(start, count)], (a, b, c), base + i))
+            if b == 0:
+                src = s["s3"].at[slot, pl.ds(start, count)]
+                dst = s["r3"].at[slot, 2 - a // 2, pl.ds(start, count)]
+            else:
+                tiles = pl.ds(1, 2) if count == 4 else pl.ds(0, 3)
+                src = s["t3"].at[slot, tiles]
+                dst = s["q3"].at[slot, 2 - a // 2, 0 if b == 2 else 1, tiles]
+            copies.append(copy(src, dst, (a, b, c), base + i))
         for c in copies:
             c.start()
-        s["r3"][slot, 2, 1] = s["s3"][slot]
+        s["r3"][slot, 2] = s["s3"][slot]
         return copies
 
     def land3(copies, out, slot, low, high):
-        for c in copies:
-            c.wait()
+        arrive(copies)
         row8 = lax.broadcasted_iota(jnp.int32, (8, 128), 0)
         edge = {-1: (gy < 2) & (row8 >= 6), 1: (gy >= GY - 2) & (row8 < 2)}
         others = {-6: (-2, gx < 4), -2: (0, gx < 2), 3: (0, gx >= GX - 2), 7: (2, gx >= GX - 4)}
@@ -353,11 +405,18 @@
             x = p - 10
             a = -4 if x < -5 else -2 if x < -1 else 0 if x < 3 else 2 if x < 7 else 4
 
+            def tile(a, b):
+                q = x - 2 * a + 2
+                if b == 0:
+                    return s["r3"][slot, 2 + a // 2, q]
+                i = [q in pair for pair in PAIRS].index(True)
+                return pltpu.roll(s["q3"][slot, 2 + a // 2, 0 if b < 0 else 1, i], 112 if q == PAIRS[i][0] else 48, 1)
+
             def part(b):
-                v = s["r3"][slot, 2 + a // 2, 1 + b, x - 2 * a + 2]
+                v = tile(a, b)
                 if x in others:
                     near, when = others[x]
-                    v = jnp.where(when, s["r3"][slot, 2 + near // 2, 1 + b, x - 2 * near + 2], v)
+                    v = jnp.where(when, tile(near, b), v)
                 return v
             middle = part(0)
             more = pltpu.roll(middle, 80, 1)
@@ -373,49 +432,60 @@
             rep[pl.ds(2 * keep * i + 1, keep, stride=2), :] = v
 
     base1, base2, base3 = 6 * ROUNDS, 6 * ROUNDS + 52, 6 * ROUNDS + 104
+    for i, table in enumerate(tables()):
+        tab[i] = table
     load_kap.wait()
+    pack(s["k0"], 0)
     pl.semaphore_wait(barrier, len(FACES))
     moving0 = faces(s["k0"], 0)
     to_level1(lambda x: s["k0"][1 + x, 8:40, :], s["k1"], 0)
+    clear0(s["ua"])
+    clear0(s["ub"])
     load_rhs.wait()
-    land(moving0, s["k0"], 0)
-
-    def weights0(x):
-        c, others = around0(s["k0"], x, ends(x))
-        diag = None
+    arrive(moving0)
+    land(s["k0"], 0, 0)
+    row32 = lax.broadcasted_iota(jnp.int32, (32, 128), 0)
+    for x in range(16):
+        c, others = around0(s["k0"], x)
+        end = ends(x, 0)
+        others[4] = jnp.where(lane32 == 0, end, others[4])
+        others[5] = jnp.where(lane32 == 127, end, others[5])
+        w = [0.5 * (c + other) for other in others]
+        diag = w[0] + w[1] + w[2] + w[3] + w[4] + w[5]
+        s["wz"][x] = jnp.where(lane32 == 0, w[4], jnp.where(lane32 == 127, w[5], 0.0))
+        s["wy"][x] = jnp.where(row32 == 0, w[2], jnp.where(row32 == 31, w[3], 0.0))
+        w[4] = jnp.where(lane32 == 0, 0.0, w[4])
+        w[5] = jnp.where(lane32 == 127, 0.0, w[5])
         for i in range(6):
-            weight = 0.5 * (c + others[i])
-            s["w0"][i, x] = weight
-            diag = weight if diag is None else diag + weight
+            s["w0"][i, x] = w[i]
         s["d0"][x] = diag
         inv = OMEGA / diag
         s["i0"][x] = inv
         s["ua"][1 + x, 8:40, :] = rhs[x] * inv
-    loop(0, 16, weights0)
-
+
+    pack(s["ua"], 1)
     moving0 = faces(s["ua"], 1)
-    land(moving0, s["ua"], 1)
-
-    def sweep0(src, out):
-        def plane(x):
-            c, acc = left0(src, x, ends(x))
-            out[1 + x, 8:40, :] = c + s["i0"][x] * acc
-        loop(0, 16, plane)
-
-    sweep0(s["ua"], s["ub"])
+    partial0(s["ua"])
+    arrive(moving0)
+    merge(1, 0)
+    for x in range(16):
+        s["ub"][1 + x, 8:40, :] = s["ua"][1 + x, 8:40, :] + s["i0"][x] * finish0(1, x)
+    pack(s["ub"], 2)
     moving0 = faces(s["ub"], 2)
     coefficient1 = send1(s["k1"], 0, base1)
-    land(moving0, s["ub"], 2)
-
-    def rest0(x):
-        residual[x] = left0(s["ub"], x, ends(x))[1]
-    loop(0, 16, rest0)
+    partial0(s["ub"])
+    arrive(moving0)
+    merge(2, 0)
+    for x in range(16):
+        residual[x] = finish0(2, x)
     to_level1(lambda x: residual[x], s["f1"], 1)
     moving1 = send1(s["f1"], 1, base1 + 26)
+    drain()
     land1(coefficient1, s["k1"], 0)
     to_level2(lambda i: s["k1"][1 + i], 0, 8, 0)
     coefficient2 = send2(0, base2)
     weights(L1, s["k1"], s["w1"], s["d1"], s["i1"])
+    land(s["ub"], 2, 1)
     land1(moving1, s["f1"], 1)
 
     first(s["u1a"], s["f1"], s["i1"], 1, 17)
@@ -426,6 +496,7 @@
     loop(3, 15, rest1)
     to_level2(lambda i: s["u1a"][3 + i], 1, 6, 1)
     moving2 = send2(1, base2 + 26)
+    drain()
     land2(coefficient2, s["k2"], 0)
     to_level3(lambda i: s["k2"][2 + i], 0)
     coefficient3 = send3(0, base3)
@@ -442,6 +513,7 @@
     loop(2, 14, rest2)
     to_level3(lambda i: s["u2a"][2 + i], 1)
     moving3 = send3(1, base3 + 14)
+    drain()
     land3(coefficient3, s["k3"], 0, 0, 22)
     weights(L3, s["k3"], s["w3"], s["d3"], s["i3"])
     land3(moving3, s["f3"], 1, 1, 21)
@@ -453,7 +525,7 @@
         u, v = v, u
 
     rep = s["rep"]
-    value = dot(u[8:14].reshape(6 * 24, 128), repeat_matrix(64))
+    value = dot(u[8:14].reshape(6 * 24, 128), tab[REPEAT_64])
     repeat_rows(value, 6, 24, 6, 12)
     for p in range(2, 14):
         i = p // 2 - 1
@@ -461,7 +533,7 @@
     sweep(L2, s["u2b"], s["u2a"], s["f2"], s["w2"], s["d2"], s["i2"], 3, 13)
     sweep(L2, s["u2a"], s["u2b"], s["f2"], s["w2"], s["d2"], s["i2"], 4, 12)
 
-    value = dot(s["u2b"][4:12].reshape(8 * 24, 128), repeat_matrix(96))
+    value = dot(s["u2b"][4:12].reshape(8 * 24, 128), tab[REPEAT_96])
     repeat_rows(value, 8, 24, 4, 16)
     for p in range(2, 16):
         i = (p + 7) // 2 - 4
@@ -470,11 +542,11 @@
     sweep(L1, s["u1a"], s["u1b"], s["f1"], s["w1"], s["d1"], s["i1"], 4, 14)
 
     value = s["u1b"][4:14].reshape(10 * 32, 128)
-    repeat_rows(dot(value, edge_matrix()), 10, 32, 4, 24)
+    repeat_rows(dot(value, tab[EDGES]), 10, 32, 4, 24)
     for x in range(16):
         i = (x + 10) // 2 - 4
-        s["h0"][x] = ends(x) + rep[48 * i + 8:48 * i + 40, :]
-    repeat_rows(dot(value, repeat_matrix(128)), 10, 32, 4, 24)
+        s["h0"][x] = ends(x, 1) + rep[48 * i + 8:48 * i + 40, :]
+    repeat_rows(dot(value, tab[REPEAT_128]), 10, 32, 4, 24)
     for p in range(18):
         i = (p + 9) // 2 - 4
         if p in (0, 17):
@@ -482,20 +554,27 @@
         else:
             s["ub"][p, 7:41, :] = s["ub"][p, 7:41, :] + rep[48 * i + 7:48 * i + 41, :]
 
-    def up0(x):
-        c, acc = left0(s["ub"], x, s["h0"][x])
-        s["ua"][1 + x, 8:40, :] = c + s["i0"][x] * acc
-    loop(0, 16, up0)
-    land(faces(s["ua"], 3), s["ua"], 3)
-    sweep0(s["ua"], s["ub"])
+    for x in range(16):
+        c, acc = core0(s["ub"], x)
+        s["ua"][1 + x, 8:40, :] = c + s["i0"][x] * (acc + s["wz"][x] * s["h0"][x])
+    pack(s["ua"], 3)
+    moving0 = faces(s["ua"], 3)
+    partial0(s["ua"])
+    clear0(s["ub"])
+    arrive(moving0)
+    merge(3, 0)
+    for x in range(16):
+        s["ub"][1 + x, 8:40, :] = s["ua"][1 + x, 8:40, :] + s["i0"][x] * finish0(3, x)
+    pack(s["ub"], 4)
     moving0 = faces(s["ub"], 4)
+    partial0(s["ub"])
     for x in range(16):
         pressure[x] = s["ub"][1 + x, 8:40, :]
-    land(moving0, s["ub"], 4)
-
-    def end0(x):
-        residual[x] = left0(s["ub"], x, ends(x))[1]
-    loop(0, 16, end0)
+    arrive(moving0)
+    merge(4, 0)
+    for x in range(16):
+        residual[x] = finish0(4, x)
+    drain()
 
 
 def cycle(rhs, kappa):
@@ -508,7 +587,7 @@
         out_specs=(vmem, vmem),
         scratch_shapes=[pltpu.VMEM(shape, F32) for shape in SCRATCH.values()] + [
             pltpu.SemaphoreType.DMA((COPIES,)), pltpu.SemaphoreType.DMA((COPIES,)),
-            pltpu.SemaphoreType.DMA((2,))],
+            pltpu.SemaphoreType.DMA((2,)), pltpu.VMEM((6, 128, 128), BF16)],
         compiler_params=pltpu.CompilerParams(
             collective_id=0, has_side_effects=True, vmem_limit_bytes=40 * 1024 * 1024),
         cost_estimate=pl.CostEstimate(flops=40_000_000, bytes_accessed=1_048_576, transcendentals=0),

time: 67.8 us -> 61.9 us (0.913)
  Pallas kernels: 63.7 us -> 57.7 us
    pallas_call x1, Pallas kernels: 63.7 us -> 57.7 us  [cycle(): pl.pallas_call(kernel, out_shape=(block, block), in_specs=[pl.BlockSpec(m...]
where the time goes in v3:
time: 61.9 us; the launch traced here: 61.7 us
  Pallas kernels  57.7 us (93%)
  local copies, waits for them, and re-layouts  3.3 us (5%)
  between operations  0.65 us (1%)
    pallas_call x1, Pallas kernels, cycle(): pl.pallas_call(kernel, out_shape=(block, block), in_specs=[pl.BlockSpec(m...  57.7 us
    unnamed x6, local copies, waits for them, and re-layouts  3.3 us

profile of v3, /device:TPU:1, one launch (start us, length us, event | category | flops | bytes accessed | tf_op | source)
XLA Modules:
  0.0 61.7 jit_solution(8914632909876732150)
XLA Ops:
  0.6 0.0 copy-start
  0.6 0.9 %copy-done = f32[16,32,128]{2,1,0:T(8,128)S(1)} copy-done((f32[16,32,128]{2,1,0:T(8,128)S(1)}, f32[16,32,128]{2,1,0:T(8,128)}, u32[]{:S(2)}) %copy-start) | copy-done | bytes 262168
  1.6 0.0 copy-start.1
  1.6 0.9 %copy-done.1 = f32[16,32,128]{2,1,0:T(8,128)S(1)} copy-done((f32[16,32,128]{2,1,0:T(8,128)S(1)}, f32[16,32,128]{2,1,0:T(8,128)}, u32[]{:S(2)}) %copy-start.1) | copy-done | bytes 262168
  2.5 57.7 %shard_map.41 = (f32[16,32,128]{2,1,0:T(8,128)S(1)}, f32[16,32,128]{2,1,0:T(8,128)S(1)}) custom-call(f32[16,32,128]{2,1,0:T(8,128)S(1)} %copy-done, f32[16,32,128]{2,1,0:T(8,128)S(1)} %copy-done.1), custom_call_target="tpu_custom_call" | custom-call | flops 40000000 | bytes 1048576 | tf_op jit(solution)/shard_map/pallas_call | solution.py:583
  60.3 0.7 %copy.6 = f32[16,32,128]{2,1,0:T(8,128)} copy(f32[16,32,128]{2,1,0:T(8,128)S(1)} %get-tuple-element.4) | data formatting | bytes 524288
  61.0 0.7 %copy.7 = f32[16,32,128]{2,1,0:T(8,128)} copy(f32[16,32,128]{2,1,0:T(8,128)S(1)} %get-tuple-element.5) | data formatting | bytes 524288
Async XLA Ops:
  0.6 1.0 %copy-start = (f32[16,32,128]{2,1,0:T(8,128)S(1)}, f32[16,32,128]{2,1,0:T(8,128)}, u32[]{:S(2)}) copy-start(f32[16,32,128]{2,1,0:T(8,128)} %rhs_in.1) | copy-start | bytes 786436
  1.6 0.9 %copy-start.1 = (f32[16,32,128]{2,1,0:T(8,128)S(1)}, f32[16,32,128]{2,1,0:T(8,128)}, u32[]{:S(2)}) copy-start(f32[16,32,128]{2,1,0:T(8,128)} %kap_in.1) | copy-start | bytes 786436

commit v4 on v3

--- a/solution.py
+++ b/solution.py
@@ -300,7 +300,7 @@
                 src = s["zp1"].at[slot, pl.ds(rows_src[0] - 8, rows_src[1])]
                 dst = s["zb1"].at[slot, 0 if c == 1 else 1, 1 - a, pl.ds(rows_dst, rows_src[1])]
             copies.append(copy(src, dst, (a, b, c), base + i))
-        for c in copies:
+        for c, o in sorted(zip(copies, NEAR), key=lambda e: e[1][2] != 0):
             c.start()
         return copies
 

time: 61.9 us -> 63.1 us (1.019)
  Pallas kernels: 57.7 us -> 59 us
    pallas_call x1, Pallas kernels: 57.7 us -> 59 us  [cycle(): pl.pallas_call(kernel, out_shape=(block, block), in_specs=[pl.BlockSpec(m...]
where the time goes in v4:
time: 63.1 us; the launch traced here: 62.9 us
  Pallas kernels  59 us (94%)
  local copies, waits for them, and re-layouts  3.3 us (5%)
  between operations  0.65 us (1%)
    pallas_call x1, Pallas kernels, cycle(): pl.pallas_call(kernel, out_shape=(block, block), in_specs=[pl.BlockSpec(m...  59 us
    unnamed x6, local copies, waits for them, and re-layouts  3.3 us

profile of v4, /device:TPU:1, one launch (start us, length us, event | category | flops | bytes accessed | tf_op | source)
XLA Modules:
  0.0 62.9 jit_solution(5712980099715812645)
XLA Ops:
  0.6 0.0 copy-start
  0.6 0.9 %copy-done = f32[16,32,128]{2,1,0:T(8,128)S(1)} copy-done((f32[16,32,128]{2,1,0:T(8,128)S(1)}, f32[16,32,128]{2,1,0:T(8,128)}, u32[]{:S(2)}) %copy-start) | copy-done | bytes 262168
  1.6 0.0 copy-start.1
  1.6 0.9 %copy-done.1 = f32[16,32,128]{2,1,0:T(8,128)S(1)} copy-done((f32[16,32,128]{2,1,0:T(8,128)S(1)}, f32[16,32,128]{2,1,0:T(8,128)}, u32[]{:S(2)}) %copy-start.1) | copy-done | bytes 262168
  2.5 59.0 %shard_map.41 = (f32[16,32,128]{2,1,0:T(8,128)S(1)}, f32[16,32,128]{2,1,0:T(8,128)S(1)}) custom-call(f32[16,32,128]{2,1,0:T(8,128)S(1)} %copy-done, f32[16,32,128]{2,1,0:T(8,128)S(1)} %copy-done.1), custom_call_target="tpu_custom_call" | custom-call | flops 40000000 | bytes 1048576 | tf_op jit(solution)/shard_map/pallas_call | solution.py:583
  61.5 0.7 %copy.6 = f32[16,32,128]{2,1,0:T(8,128)} copy(f32[16,32,128]{2,1,0:T(8,128)S(1)} %get-tuple-element.4) | data formatting | bytes 524288
  62.2 0.7 %copy.7 = f32[16,32,128]{2,1,0:T(8,128)} copy(f32[16,32,128]{2,1,0:T(8,128)S(1)} %get-tuple-element.5) | data formatting | bytes 524288
Async XLA Ops:
  0.6 1.0 %copy-start = (f32[16,32,128]{2,1,0:T(8,128)S(1)}, f32[16,32,128]{2,1,0:T(8,128)}, u32[]{:S(2)}) copy-start(f32[16,32,128]{2,1,0:T(8,128)} %rhs_in.1) | copy-start | bytes 786436
  1.6 0.9 %copy-start.1 = (f32[16,32,128]{2,1,0:T(8,128)S(1)}, f32[16,32,128]{2,1,0:T(8,128)}, u32[]{:S(2)}) copy-start(f32[16,32,128]{2,1,0:T(8,128)} %kap_in.1) | copy-start | bytes 786436
